TPU v7x, 512 devices: a whole 4x4x16 slice. The times are simulated.
512 devices in a mesh: seq: 32 (over z_lo, x), tp: 8 (over y, core), pool: 2 (over z_hi).
Axes of the slice: x: 4, y: 4, z: 16 (z_hi: 2, z_lo: 8; z = z_hi * 8 + z_lo), core: 2. Of those that a mesh axis runs over, the one named last changes fastest.
Arguments:
- q_pre: bfloat16 [2, 4096, 8192], P('pool', 'seq', 'tp'), may hold values from -102 to 102
- k_pre: bfloat16 [2, 4096, 1024], P('pool', 'seq', 'tp'), may hold values from -10 to 10
- v_pre: bfloat16 [2, 4096, 1024], P('pool', 'seq', 'tp'), may hold values from -6 to 6
- out_weight: bfloat16 [8192, 12288], P('tp', 'seq'), may hold values from -0.0625 to 0.0625
- residual: bfloat16 [2, 4096, 12288], P('pool', 'tp', 'seq'), may hold values from -6 to 6
- span_ids: int32 [2, 32], replicated, may hold values from 0 to 31, each once within a row
- page_counts: int32 [2, 8], replicated, may hold values from 1 to 16, 32 in all within a row
- tail_rows: int32 [2, 8], replicated, may hold values from 1 to 128
- dest_group: int32 [2, 8], replicated, may hold values from 0 to 31, as said below
- dec_q: bfloat16 [2, 8, 4, 8192], P(None, None, None, 'tp'), may hold values from -102 to 102
- dec_k: bfloat16 [2, 8, 4, 1024], P(None, None, None, 'tp'), may hold values from -10 to 10
- dec_v: bfloat16 [2, 8, 4, 1024], P(None, None, None, 'tp'), may hold values from -6 to 6
Outputs:
- mixed: bfloat16 [2, 4096, 12288], P('pool', 'tp', 'seq')
- decoded: bfloat16 [2, 32, 4, 8192], P('pool', 'seq', None, 'tp')
Inputs may be any that keep to these rules, and one draw needn't show every extreme that they name: `dest_group`: distinct within a row; 0 and 31 are in every row.
All inputs are finite; a program needn't handle non-finite values.
Results may differ from a plain program's by a relative error of at most 0.01.
Values may be sent and summed in bfloat16 or wider, within the bound.
A program may use at most 64 MiB of HBM per device.

v0:
```python
import math

import jax
import jax.numpy as jnp
from jax import lax
from jax.sharding import PartitionSpec as P

HD = 128
QH = 64
KVH = 8


NEG_FILL = -1e30


def swapped(block, axis, distance):
    count = lax.axis_size(axis)
    route = []
    for low in range(count):
        high = low | 1 << distance
        if high != low and high < count:
            route += [(low, high), (high, low)]
    return lax.ppermute(block, axis, route)


def span_request(counts, page_pos):
    ends_incl = jnp.cumsum(counts)
    return jnp.sum((ends_incl <= page_pos).astype(jnp.int32))


def pick_row(table, index):
    return lax.dynamic_index_in_dim(table, index, 0, keepdims=False)


def per_device(
    q_pre,
    k_pre,
    v_pre,
    out_weight,
    residual,
    span_ids,
    page_counts,
    tail_rows,
    dest_group,
    dec_q,
    dec_k,
    dec_v,
):
    pool_at = lax.axis_index("pool")
    seq_at = lax.axis_index("seq")
    tp_count = lax.axis_size("tp")
    repeat = QH // KVH
    span_len = q_pre.shape[1]
    groups = k_pre.shape[2] // HD
    score_scale = 1.0 / math.sqrt(HD)
    local_ids = pick_row(span_ids, pool_at)
    local_counts = pick_row(page_counts, pool_at)
    own_page = pick_row(local_ids, seq_at)
    row_index = jnp.arange(span_len, dtype=jnp.int32)
    query_pos = own_page * span_len + row_index
    query_req = span_request(local_counts, own_page)
    queries = q_pre[0].reshape(span_len, groups, repeat, HD)
    keys_here = k_pre[0]
    values_here = v_pre[0]

    def attend_shard(state, shard_keys, shard_values, device):
        page_pos = pick_row(local_ids, device)
        key_pos = page_pos * span_len + row_index
        visible = (span_request(local_counts, page_pos) == query_req) & (
            key_pos[None, :] <= query_pos[:, None]
        )
        visible = visible[:, None, None, :]
        highest, weight_sum, accum = state
        scores = (
            jnp.einsum(
                "qgrd,kgd->qgrk",
                queries,
                shard_keys.reshape(span_len, groups, HD),
                preferred_element_type=jnp.float32,
            )
            * score_scale
        )
        scores = jnp.where(visible, scores, NEG_FILL)
        new_high = jnp.maximum(highest, jnp.max(scores, axis=3))
        weights = jnp.where(visible, jnp.exp(scores - new_high[..., None]), 0.0)
        factor = jnp.exp(highest - new_high)
        weight_sum = weight_sum * factor + jnp.sum(weights, axis=3)
        accum = accum * factor[..., None] + jnp.einsum(
            "qgrk,kgd->qgrd",
            weights.astype(jnp.bfloat16),
            shard_values.reshape(span_len, groups, HD),
            preferred_element_type=jnp.float32,
        )
        return (new_high, weight_sum, accum)

    initial = (
        jnp.full((span_len, groups, repeat), NEG_FILL, jnp.float32),
        jnp.zeros((span_len, groups, repeat), jnp.float32),
        jnp.zeros((span_len, groups, repeat, HD), jnp.float32),
    )
    piece_keys = lax.all_gather(keys_here, "seq", axis=0, tiled=True)
    piece_values = lax.all_gather(values_here, "seq", axis=0, tiled=True)

    def per_shard(shard_no, inner):
        shard_keys = lax.dynamic_slice_in_dim(piece_keys, shard_no * span_len, span_len, 0)
        shard_values = lax.dynamic_slice_in_dim(piece_values, shard_no * span_len, span_len, 0)
        return attend_shard(inner, shard_keys, shard_values, shard_no)

    final_state = lax.fori_loop(0, piece_keys.shape[0] // span_len, per_shard, initial)
    attention = (
        (final_state[2] / final_state[1][..., None]).reshape(span_len, -1).astype(jnp.bfloat16)
    )
    tok_rows = residual.shape[1]
    partial_rows = jnp.dot(
        lax.all_gather(attention, "seq", axis=0, tiled=True),
        out_weight,
        preferred_element_type=jnp.float32,
    ).astype(jnp.bfloat16)
    arrived = lax.all_to_all(
        partial_rows.reshape(tp_count, tok_rows, -1), "tp", split_axis=0, concat_axis=0, tiled=True
    )
    summed = arrived[0].astype(jnp.float32)
    for source in range(1, tp_count):
        summed = summed + arrived[source].astype(jnp.float32)
    mixed = (summed + residual[0].astype(jnp.float32)).astype(jnp.bfloat16)[None]
    other_pool = 1 - pool_at
    pages = jnp.stack([keys_here, values_here])
    crossed = swapped(pages, "pool", 0)
    far_ids = pick_row(span_ids, other_pool)
    far_counts = pick_row(page_counts, other_pool)
    far_tails = pick_row(tail_rows, other_pool)
    far_dest = pick_row(dest_group, other_pool)
    matched = far_dest == seq_at
    holds_one = jnp.any(matched)
    chosen = jnp.sum(jnp.where(matched, jnp.arange(far_dest.shape[0], dtype=jnp.int32), 0))
    chosen_len = pick_row(far_counts, chosen)
    first_page = pick_row(jnp.cumsum(far_counts), chosen) - chosen_len
    live_rows = (chosen_len - 1) * span_len + pick_row(far_tails, chosen)
    most_pages = lax.axis_size("seq") // 2
    empty_cache = jnp.zeros((2, most_pages * span_len, keys_here.shape[1]), jnp.bfloat16)
    piece = lax.all_gather(crossed, "seq", axis=1, tiled=True)

    def place_one(shard_no, inner):
        shard = lax.dynamic_slice_in_dim(piece, shard_no * span_len, span_len, 1)
        page_pos = pick_row(far_ids, shard_no)
        owner = span_request(far_counts, page_pos)
        slot_no = jnp.clip(page_pos - first_page, 0, most_pages - 1)
        written = lax.dynamic_update_slice_in_dim(inner, shard, slot_no * span_len, 1)
        return jnp.where(holds_one & (owner == chosen), written, inner)

    cache = lax.fori_loop(0, piece.shape[1] // span_len, place_one, empty_cache)
    steps_count = dec_q.shape[2]
    query_rows = pick_row(pick_row(dec_q, other_pool), chosen).reshape(
        steps_count, groups, repeat, HD
    )
    new_keys = pick_row(pick_row(dec_k, other_pool), chosen).reshape(steps_count, groups, HD)
    new_values = pick_row(pick_row(dec_v, other_pool), chosen).reshape(steps_count, groups, HD)
    cache_keys = cache[0].reshape(-1, groups, HD)
    cache_values = cache[1].reshape(-1, groups, HD)
    slot_rows = jnp.arange(cache_keys.shape[0], dtype=jnp.int32)
    live_mask = (slot_rows < live_rows)[None, None, None, :]
    steps_at = jnp.arange(steps_count, dtype=jnp.int32)
    causal = (steps_at[None, :] <= steps_at[:, None])[:, None, None, :]
    old_scores = (
        jnp.einsum("sgrd,tgd->sgrt", query_rows, cache_keys, preferred_element_type=jnp.float32)
        * score_scale
    )
    old_scores = jnp.where(live_mask, old_scores, NEG_FILL)
    new_scores = (
        jnp.einsum("sgrd,jgd->sgrj", query_rows, new_keys, preferred_element_type=jnp.float32)
        * score_scale
    )
    new_scores = jnp.where(causal, new_scores, NEG_FILL)
    highest = jnp.maximum(jnp.max(old_scores, axis=3), jnp.max(new_scores, axis=3))[..., None]
    old_weights = jnp.where(live_mask, jnp.exp(old_scores - highest), 0.0)
    new_weights = jnp.where(causal, jnp.exp(new_scores - highest), 0.0)
    denominator = jnp.sum(old_weights, axis=3, keepdims=True) + jnp.sum(
        new_weights, axis=3, keepdims=True
    )
    result = (
        jnp.einsum(
            "sgrt,tgd->sgrd",
            old_weights.astype(jnp.bfloat16),
            cache_values,
            preferred_element_type=jnp.float32,
        )
        + jnp.einsum(
            "sgrj,jgd->sgrd",
            new_weights.astype(jnp.bfloat16),
            new_values,
            preferred_element_type=jnp.float32,
        )
    ) / denominator
    decoded = jnp.where(holds_one, result, 0.0).reshape(1, 1, steps_count, -1).astype(jnp.bfloat16)
    return (mixed, decoded)


def solution(mesh):
    placed = (
        P("pool", "seq", "tp"),
        P("pool", "seq", "tp"),
        P("pool", "seq", "tp"),
        P("tp", "seq"),
        P("pool", "tp", "seq"),
        P(),
        P(),
        P(),
        P(),
        P(None, None, None, "tp"),
        P(None, None, None, "tp"),
        P(None, None, None, "tp"),
    )
    return jax.shard_map(
        per_device,
        mesh=mesh,
        in_specs=placed,
        out_specs=(P("pool", "tp", "seq"), P("pool", "seq", None, "tp")),
        check_vma=False,
    )
```

profile of v0, /device:TPU:24, one launch (start us, length us, event | category | flops | bytes accessed | tf_op | source)
XLA Modules:
  0.0 1241.4 jit_solution(11114491601064989076)
XLA Ops:
  8.0 1.5 copy.22
  15.7 220.6 %all-gather.11.cloned.1.call-done = bf16[1,4096,128]{2,1,0:T(8,128)(2,1)} async-done(((bf16[1,128,128]{2,1,0:T(8,128)(2,1)}), bf16[1,4096,128]{2,1,0:T(8,128)(2,1)}) %all-gather.11.cloned.1.call-update) | async-done | bytes 1048592 | tf_op jit(solution)/shard_map/all_gather | solution.py:101
  236.3 178.4 %all-gather.13.cloned.1.call-done = bf16[1,4096,128]{1,2,0:T(8,128)(2,1)} async-done(((bf16[1,128,128]{1,2,0:T(8,128)(2,1)}), bf16[1,4096,128]{1,2,0:T(8,128)(2,1)}) %all-gather.13.cloned.1.call-update) | async-done | bytes 1048592 | tf_op jit(solution)/shard_map/all_gather | solution.py:102
  414.7 197.4 %while.36 = (s32[]{:T(128)}, f32[128,1,8]{0,2,1:T(8,128)S(1)}, f32[128,1,8]{0,2,1:T(8,128)S(1)}, f32[128,1,8,128]{0,3,2,1:T(8,128)S(1)}, s32[32]{0:T(128)S(1)}, ...) while((s32[]{:T(128)}, f32[128,1,8]{0,2,1:T(8,128)S(1)}, ...), condition=%wide.region_6.7_spmd.clone, body=%wide.region_2.6_spmd.clone.sunk | while | flops 68720928 | bytes 3082537 | solution.py:109
  416.0 1.3 fusion.81
  422.2 1.3 fusion.81
  428.4 1.3 fusion.81
  434.5 1.3 fusion.81
  440.7 1.3 fusion.81
  446.9 1.3 fusion.81
  453.0 1.3 fusion.81
  459.2 1.3 fusion.81
  465.4 1.3 fusion.81
  520.9 1.3 fusion.81
  539.4 1.3 fusion.81
  613.0 5.2 collective-permute-start
  618.2 9.7 collective-permute-done
  636.9 180.4 %all-gather.7.cloned.1.call-done = bf16[4096,1024]{0,1:T(8,128)(2,1)} async-done(((bf16[128,1024]{0,1:T(8,128)(2,1)}), bf16[4096,1024]{0,1:T(8,128)(2,1)}) %all-gather.7.cloned.1.call-update) | async-done | bytes 8388624 | tf_op jit(solution)/shard_map/all_gather | solution.py:115
  817.3 9.5 convolution_convert_fusion
  826.8 4.8 all-to-all-start
  831.7 209.5 %all-gather.9.cloned.1.call-done = bf16[2,4096,128]{2,1,0:T(8,128)(2,1)} async-done(((bf16[2,128,128]{2,1,0:T(8,128)(2,1)}), bf16[2,4096,128]{2,1,0:T(8,128)(2,1)}) %all-gather.9.cloned.1.call-update) | async-done | bytes 2097168 | tf_op jit(solution)/shard_map/all_gather | solution.py:141
  1041.3 187.5 %while.35 = (s32[]{:T(128)}, bf16[2,2048,128]{2,1,0:T(8,128)(2,1)S(1)}, s32[32]{0:T(128)S(1)}, s32[8,1]{0,1:T(1,128)S(1)}, s32[]{:T(128)}, /*index=5*/pred[]{:T(...) while((s32[]{:T(128)}, ...), condition=%wide.region_12.13_spmd, body=%wide.region_10.12_spmd.sunk | while | flops 32806 | bytes 196950 | solution.py:151
  1229.7 1.5 fusion.32
  1231.8 3.0 add_convert_fusion
  (461 shorter events, 223.2 us)
Async XLA Ops:
  7.2 810.1 %copy-start = (bf16[1024,384]{1,0:T(8,128)(2,1)S(1)}, bf16[1024,384]{1,0:T(8,128)(2,1)}, u32[]{:S(2)}) copy-start(bf16[1024,384]{1,0:T(8,128)(2,1)} %param.19) | copy-start | bytes 2359300
  7.2 229.2 %all-gather.11.cloned.1.call-start = ((), (), s32[]{:S(2)}) async-start(), calls=%async_computation.3 | async-start | bytes 1081344 | tf_op jit(solution)/shard_map/all_gather | solution.py:101
  7.9 406.8 %all-gather.13.cloned.1.call-start = ((), (), s32[]{:S(2)}) async-start(), calls=%async_computation.4 | async-start | bytes 1081344 | tf_op jit(solution)/shard_map/all_gather | solution.py:102
  9.5 807.8 %all-gather.7.cloned.1.call-start = ((), (), s32[]{:S(2)}) async-start(), calls=%async_computation.1 | async-start | bytes 8650752 | tf_op jit(solution)/shard_map/all_gather | solution.py:115
  414.7 198.2 %copy-start.2 = (bf16[1,128,128]{2,1,0:T(8,128)(2,1)S(1)}, bf16[1,128,128]{2,1,0:T(8,128)(2,1)}, u32[]{:S(2)}) copy-start(bf16[1,128,128]{2,1,0:T(8,128)(2,1)} %param.17) | copy-start | bytes 98308
  414.7 198.3 %copy-start.3 = (bf16[1,128,128]{2,1,0:T(8,128)(2,1)S(1)}, bf16[1,128,128]{2,1,0:T(8,128)(2,1)}, u32[]{:S(2)}) copy-start(bf16[1,128,128]{2,1,0:T(8,128)(2,1)} %param.18) | copy-start | bytes 98308
  414.7 214.0 %copy-start.6 = (s32[2,8]{1,0:T(2,128)S(1)}, s32[2,8]{1,0:T(2,128)}, u32[]{:S(2)}) copy-start(s32[2,8]{1,0:T(2,128)} %param.24) | copy-start | bytes 196
  414.7 216.2 %copy-start.5 = (s32[2,8]{1,0:T(2,128)S(1)}, s32[2,8]{1,0:T(2,128)}, u32[]{:S(2)}) copy-start(s32[2,8]{1,0:T(2,128)} %param.22) | copy-start | bytes 196
  414.7 218.6 %copy-start.7 = (s32[2,8]{1,0:T(2,128)S(1)}, s32[2,8]{1,0:T(2,128)}, u32[]{:S(2)}) copy-start(s32[2,8]{1,0:T(2,128)} %param.23) | copy-start | bytes 196
  612.9 428.2 %all-gather.9.cloned.1.call-start = ((), (), s32[]{:S(2)}) async-start(), calls=%async_computation.2 | async-start | bytes 2162688 | tf_op jit(solution)/shard_map/all_gather | solution.py:141
  613.0 14.9 %collective-permute-start = (bf16[2,128,128]{2,1,0:T(8,128)(2,1)S(1)}, bf16[2,128,128]{2,1,0:T(8,128)(2,1)S(1)}, u32[]{:S(2)}, u32[]{:S(2)}) collective-permute-start(bf16[2,128,128]{2,1,0:T(8,128)(2,1)S(1)} %pad_maximum_fusion), channel_id=1, source_target_pairs={{0,1},{1,0},{2,3},{3,2},{4,5},{5,4},{6,7},{7,6},{8,9},{9,8},{10,11... | collective-permute-start | bytes 196616 | tf_op jit(solution)/shard_map/ppermute | solution.py:23
  627.9 0.6 copy-start.4
  826.8 405.0 %all-to-all-start = ((bf16[8,512,384]{2,1,0:T(8,128)(2,1)}), bf16[8,512,384]{2,1,0:T(8,128)(2,1)}, u32[]{:S(2)}, u32[]{:S(2)}) async-start(bf16[8,512,384]{2,1,0:T(8,128)(2,1)} %bitcast.155), calls=%async_computation | async-start | bytes 6291456 | tf_op jit(solution)/shard_map/all_to_all | solution.py:119
  831.7 400.2 %copy-start.1 = (bf16[1,512,384]{2,1,0:T(8,128)(2,1)S(1)}, bf16[1,512,384]{2,1,0:T(8,128)(2,1)}, u32[]{:S(2)}) copy-start(bf16[1,512,384]{2,1,0:T(8,128)(2,1)} %param.20) | copy-start | bytes 1179652
Sparse Core Ops, SparseCore 0:
  10.1 226.2 all-gather.10
  238.9 175.7 all-gather.12
  613.0 204.1 all-gather.6
  819.2 221.8 all-gather.8
where the time goes:
time: 1250 us; the launch traced here: 1240 us
  waiting for transfers between devices  799 us (64%)
  loops' own time  163 us (13%)
  other arithmetic  126 us (10%)
  matrix products  79.7 us (6%)
  local copies, waits for them, and re-layouts  46.5 us (4%)
  between operations  17.4 us (1%)
    all_gather x1, waiting for transfers between devices, per_device(): piece_keys = lax.all_gather(keys_here, 'seq', axis=0, tiled=True)  221 us
    all_gather x1, waiting for transfers between devices, per_device(): piece = lax.all_gather(crossed, 'seq', axis=1, tiled=True)  210 us
    all_gather x1, waiting for transfers between devices, per_device(): lax.all_gather(attention, 'seq', axis=0, tiled=True)  180 us
    all_gather x1, waiting for transfers between devices, per_device(): piece_values = lax.all_gather(values_here, 'seq', axis=0, tiled=True)  178 us
    another operation x1, loops' own time, per_device(): cache = lax.fori_loop(0, piece.shape[1] // span_len, place_one, empty_cache)  99.5 us
    reduce_sum x65, other arithmetic, span_request(): return jnp.sum((ends_incl <= page_pos).astype(jnp.int32))  83.4 us
    another operation x1, loops' own time, per_device(): lax.fori_loop(0, piece_keys.shape[0] // span_len, per_shard, initial)  63.1 us
    dynamic_slice x67, local copies, waits for them, and re-layouts, pick_row(): return lax.dynamic_index_in_dim(table, index, 0, keepdims=False)  40 us
  transfers between devices with their start and end apart: 6, of which 5 were waited for; matrix products, arithmetic and copies ran while one was open for 9% of the time, Pallas kernels for 0%

commit v1 on v0

v1 whole, which is shorter than its diff:
```python
import functools
import math

import jax
import jax.numpy as jnp
from jax import lax
from jax.experimental import pallas as pl
from jax.experimental.pallas import tpu as pltpu
from jax.sharding import PartitionSpec as P

HD = 128
QH = 64
KVH = 8
X_SIZE = 4
NEG_FILL = -1e30
LOG2E = 1.4426950408889634
MESH = pl.DeviceIdType.MESH
F32 = jnp.float32
BF16 = jnp.bfloat16


def remote(src, dst, send_sem, recv_sem, seq):
    return pltpu.make_async_remote_copy(
        src_ref=src,
        dst_ref=dst,
        send_sem=send_sem,
        recv_sem=recv_sem,
        device_id={"seq": seq},
        device_id_type=MESH,
    )


def gather_kernel(
    nz, first_ref, second_ref, out_ref, z_send, z_recv, x_send, x_recv, far_send, far_recv
):
    me = lax.axis_index("seq")
    z, x = me // X_SIZE, me % X_SIZE
    right = z * X_SIZE + (x + 1) % X_SIZE
    left = z * X_SIZE + (x + 3) % X_SIZE
    opposite = (x + 2) % X_SIZE

    barrier = pltpu.get_barrier_semaphore()
    for seq in (right, left):
        pl.semaphore_signal(barrier, inc=1, device_id={"seq": seq}, device_id_type=MESH)

    @pl.when(z > 0)
    def _():
        pl.semaphore_signal(barrier, inc=1, device_id={"seq": me - X_SIZE}, device_id_type=MESH)

    @pl.when(z < nz - 1)
    def _():
        pl.semaphore_signal(barrier, inc=1, device_id={"seq": me + X_SIZE}, device_id_type=MESH)

    out_ref[me, 0] = first_ref[...]
    out_ref[me, 1] = second_ref[...]
    peers = 2 + jnp.where(z > 0, 1, 0) + jnp.where(z < nz - 1, 1, 0)
    pl.semaphore_wait(barrier, peers)

    def z_copy(block_z, direction, target):
        slot = out_ref.at[block_z * X_SIZE + x]
        return remote(slot, slot, z_send.at[direction, block_z], z_recv.at[block_z], target)

    def x_copy(block_z, block_x, direction, target):
        slot = out_ref.at[block_z * X_SIZE + block_x]
        return remote(
            slot, slot, x_send.at[direction, block_z], x_recv.at[direction, block_z], target
        )

    def far_copy(block_z, block_x, direction, target):
        slot = out_ref.at[block_z * X_SIZE + block_x, direction]
        return remote(
            slot, slot, far_send.at[direction, block_z], far_recv.at[direction, block_z], target
        )

    def spread(block_z):
        x_copy(block_z, x, 0, right).start()
        x_copy(block_z, x, 1, left).start()

    def relay(block_z):
        x_copy(block_z, (x + 3) % X_SIZE, 0, right).wait_recv()
        far_copy(block_z, (x + 3) % X_SIZE, 0, right).start()
        x_copy(block_z, (x + 1) % X_SIZE, 1, left).wait_recv()
        far_copy(block_z, (x + 1) % X_SIZE, 1, left).start()

    def step(t, carry):
        low, high = z - t, z + t

        @pl.when((t > 0) & (low >= 0))
        def _():
            z_copy(low, 0, me).wait_recv()

        @pl.when((low >= 0) & (z < nz - 1))
        def _():
            z_copy(low, 0, me + X_SIZE).start()

        @pl.when((t > 0) & (high < nz))
        def _():
            z_copy(high, 1, me).wait_recv()

        @pl.when((high < nz) & (z > 0))
        def _():
            z_copy(high, 1, me - X_SIZE).start()

        @pl.when(low >= 0)
        def _():
            spread(low)

        @pl.when((t > 0) & (high < nz))
        def _():
            spread(high)

        @pl.when((t > 0) & (low + 1 >= 0))
        def _():
            relay(low + 1)

        @pl.when((t > 1) & (high - 1 < nz))
        def _():
            relay(high - 1)

        return carry

    lax.fori_loop(0, nz + 1, step, 0)

    def drain(block_z, carry):
        @pl.when((block_z <= z) & (z < nz - 1))
        def _():
            z_copy(block_z, 0, me).wait_send()

        @pl.when((block_z >= z) & (z > 0))
        def _():
            z_copy(block_z, 1, me).wait_send()

        x_copy(block_z, x, 0, right).wait_send()
        x_copy(block_z, x, 1, left).wait_send()
        far_copy(block_z, opposite, 0, right).wait()
        far_copy(block_z, opposite, 1, left).wait()
        return carry

    lax.fori_loop(0, nz, drain, 0)


def gather_seq(first, second, count, collective_id):
    nz = count // X_SIZE
    rows, columns = first.shape
    dma = pltpu.SemaphoreType.DMA
    return pl.pallas_call(
        functools.partial(gather_kernel, nz),
        out_shape=jax.ShapeDtypeStruct((count, 2, rows, columns), first.dtype),
        in_specs=[pl.BlockSpec(memory_space=pltpu.VMEM)] * 2,
        out_specs=pl.BlockSpec(memory_space=pltpu.VMEM),
        scratch_shapes=[dma((2, nz)), dma((nz,)), dma((2, nz)), dma((2, nz)), dma((2, nz)), dma((2, nz))],
        compiler_params=pltpu.CompilerParams(
            collective_id=collective_id, has_side_effects=True, vmem_limit_bytes=40 << 20
        ),
    )(first, second)


def matmul_nt(a, b):
    return lax.dot_general(a, b, (((1,), (1,)), ((), ())), preferred_element_type=F32)


def matmul_tn(a, b):
    return lax.dot_general(a, b, (((0,), (0,)), ((), ())), preferred_element_type=F32)


CHUNK = 4


def attend_kernel(
    span_ref,
    counts_ref,
    tails_ref,
    dest_ref,
    q_ref,
    kv_ref,
    dq_ref,
    dk_ref,
    dv_ref,
    out_ref,
    dec_ref,
    place,
    dec_rows,
    new_page,
):
    pool_at = lax.axis_index("pool")
    seq_at = lax.axis_index("seq")
    pages, span = kv_ref.shape[0], kv_ref.shape[2]
    requests = counts_ref.shape[1]
    steps = dec_ref.shape[0]
    repeat = QH // KVH
    factor = LOG2E / math.sqrt(HD)
    keys = CHUNK * span

    def invert(j, carry):
        place[span_ref[pool_at, j]] = j
        return carry

    lax.fori_loop(0, pages, invert, 0)

    own = span_ref[pool_at, seq_at]
    begin = jnp.int32(0)
    first = jnp.int32(0)
    dec_first, dec_count, dec_tail, dec_no, holds = (jnp.int32(0),) * 5
    for r in range(requests):
        count = counts_ref[pool_at, r]
        first = jnp.where(begin <= own, begin, first)
        match = dest_ref[pool_at, r] == seq_at
        dec_first = jnp.where(match, begin, dec_first)
        dec_count = jnp.where(match, count, dec_count)
        dec_tail = jnp.where(match, tails_ref[pool_at, r], dec_tail)
        dec_no = jnp.where(match, r, dec_no)
        holds = jnp.where(match, 1, holds)
        begin = begin + count

    def load(which, page, last):
        return jnp.concatenate(
            [kv_ref[place[jnp.minimum(page + j, last)], which] for j in range(CHUNK)], axis=0
        )

    last_chunk = (own - first) // CHUNK
    width = 2 * HD
    ahead = lax.broadcasted_iota(jnp.int32, (keys, width), 0) - (
        lax.broadcasted_iota(jnp.int32, (keys, width), 1) % span
    )
    visible = ahead <= (own - first - last_chunk * CHUNK) * span
    for pair in range(repeat // 2):
        heads = [2 * pair, 2 * pair + 1]
        rows = jnp.concatenate([q_ref[:, h * HD : (h + 1) * HD] for h in heads], axis=0)

        page = first + last_chunk * CHUNK
        scores = jnp.where(visible, matmul_nt(load(0, page, own), rows), NEG_FILL)
        highest = jnp.max(scores, axis=0, keepdims=True)
        weights = jnp.exp2((scores - highest) * factor)
        total = jnp.sum(weights, axis=0, keepdims=True)
        accum = matmul_tn(load(1, page, own), weights.astype(BF16))

        def chunk(i, state):
            highest, total, accum = state
            page = first + i * CHUNK
            scores = matmul_nt(load(0, page, own), rows)
            new_high = jnp.maximum(highest, jnp.max(scores, axis=0, keepdims=True))
            weights = jnp.exp2((scores - new_high) * factor)
            fade = jnp.exp2((highest - new_high) * factor)
            total = total * fade + jnp.sum(weights, axis=0, keepdims=True)
            accum = accum * fade + matmul_tn(load(1, page, own), weights.astype(BF16))
            return (new_high, total, accum)

        highest, total, accum = lax.fori_loop(0, last_chunk, chunk, (highest, total, accum))
        result = accum / total
        for n, h in enumerate(heads):
            out_ref[:, h * HD : (h + 1) * HD] = jnp.transpose(
                result[:, n * HD : (n + 1) * HD]
            ).astype(BF16)

    @pl.when(holds == 0)
    def _():
        dec_ref[...] = jnp.zeros_like(dec_ref)

    @pl.when(holds == 1)
    def _():
        queries = dq_ref[pool_at, dec_no].astype(F32)
        for h in range(repeat):
            dec_rows[h * steps : (h + 1) * steps, :] = queries[:, h * HD : (h + 1) * HD]
        rows = dec_rows[...].astype(BF16)
        new_page[...] = jnp.zeros_like(new_page)
        new_page[0, :steps, :] = dk_ref[pool_at, dec_no].astype(F32)
        new_page[1, :steps, :] = dv_ref[pool_at, dec_no].astype(F32)

        count = rows.shape[0]
        step_of = lax.broadcasted_iota(jnp.int32, (count, span), 0) % steps
        causal = lax.broadcasted_iota(jnp.int32, (count, span), 1) <= step_of
        scores = jnp.where(causal, matmul_nt(rows, new_page[0].astype(BF16)), NEG_FILL)
        highest = jnp.max(scores, axis=1, keepdims=True)
        weights = jnp.exp2((scores - highest) * factor)
        total = jnp.sum(weights, axis=1, keepdims=True)
        accum = jnp.dot(
            weights.astype(BF16), new_page[1].astype(BF16), preferred_element_type=F32
        )
        live = (dec_count - 1) * span + dec_tail
        last = dec_first + dec_count - 1
        key_no = lax.broadcasted_iota(jnp.int32, (count, keys), 1)

        def chunk(i, state):
            highest, total, accum = state
            page = dec_first + i * CHUNK
            scores = matmul_nt(rows, load(0, page, last))
            scores = jnp.where(key_no < live - i * keys, scores, NEG_FILL)
            new_high = jnp.maximum(highest, jnp.max(scores, axis=1, keepdims=True))
            weights = jnp.exp2((scores - new_high) * factor)
            fade = jnp.exp2((highest - new_high) * factor)
            total = total * fade + jnp.sum(weights, axis=1, keepdims=True)
            accum = accum * fade + jnp.dot(
                weights.astype(BF16), load(1, page, last), preferred_element_type=F32
            )
            return (new_high, total, accum)

        state = lax.fori_loop(0, (dec_count + CHUNK - 1) // CHUNK, chunk, (highest, total, accum))
        dec_rows[...] = state[2] / state[1]
        for h in range(repeat):
            dec_ref[:, h * HD : (h + 1) * HD] = dec_rows[h * steps : (h + 1) * steps, :].astype(
                BF16
            )


def attend(span_ids, page_counts, tail_rows, dest_group, q, kv, dec_q, dec_k, dec_v):
    steps = dec_q.shape[2]
    span = q.shape[0]
    smem = pl.BlockSpec(memory_space=pltpu.SMEM)
    vmem = pl.BlockSpec(memory_space=pltpu.VMEM)
    return pl.pallas_call(
        attend_kernel,
        out_shape=(
            jax.ShapeDtypeStruct(q.shape, BF16),
            jax.ShapeDtypeStruct((steps, q.shape[1]), BF16),
        ),
        in_specs=[smem] * 4 + [vmem] * 5,
        out_specs=(vmem, vmem),
        scratch_shapes=[
            pltpu.SMEM((kv.shape[0],), jnp.int32),
            pltpu.VMEM((steps * (QH // KVH), HD), F32),
            pltpu.VMEM((2, span, HD), F32),
        ],
        compiler_params=pltpu.CompilerParams(vmem_limit_bytes=40 << 20),
    )(span_ids, page_counts, tail_rows, dest_group, q, kv, dec_q, dec_k, dec_v)


def per_device(
    q_pre,
    k_pre,
    v_pre,
    out_weight,
    residual,
    span_ids,
    page_counts,
    tail_rows,
    dest_group,
    dec_q,
    dec_k,
    dec_v,
):
    seq_count = lax.axis_size("seq")
    tp_count = lax.axis_size("tp")
    kv = gather_seq(k_pre[0], v_pre[0], seq_count, 0)
    attention, answers = attend(
        span_ids, page_counts, tail_rows, dest_group, q_pre[0], kv, dec_q, dec_k, dec_v
    )
    decoded = lax.ppermute(answers, "pool", [(0, 1), (1, 0)])[None, None]

    half = attention.shape[0] // 2
    rows = gather_seq(attention[:half], attention[half:], seq_count, 1)
    partial_rows = jnp.dot(
        rows.reshape(-1, rows.shape[3]), out_weight, preferred_element_type=F32
    ).astype(BF16)
    tok_rows = residual.shape[1]
    arrived = lax.all_to_all(
        partial_rows.reshape(tp_count, tok_rows, -1), "tp", split_axis=0, concat_axis=0, tiled=True
    )
    summed = arrived[0].astype(F32)
    for source in range(1, tp_count):
        summed = summed + arrived[source].astype(F32)
    mixed = (summed + residual[0].astype(F32)).astype(BF16)[None]
    return (mixed, decoded)


def solution(mesh):
    placed = (
        P("pool", "seq", "tp"),
        P("pool", "seq", "tp"),
        P("pool", "seq", "tp"),
        P("tp", "seq"),
        P("pool", "tp", "seq"),
        P(),
        P(),
        P(),
        P(),
        P(None, None, None, "tp"),
        P(None, None, None, "tp"),
        P(None, None, None, "tp"),
    )
    return jax.shard_map(
        per_device,
        mesh=mesh,
        in_specs=placed,
        out_specs=(P("pool", "tp", "seq"), P("pool", "seq", None, "tp")),
        check_vma=False,
    )
```

time: 1250 us -> 179 us (0.14)
  waiting for transfers between devices: 799 us -> 23.1 us
  loops' own time: 163 us -> 0 us
  other arithmetic: 126 us -> 3.03 us
  Pallas kernels: 0 us -> 117 us
  matrix products: 79.7 us -> 5.92 us
  local copies, waits for them, and re-layouts: 46.5 us -> 8.21 us
  between operations: 17.4 us -> 0.71 us
    all_gather x4 -> x0, waiting for transfers between devices: 789 us -> none  [the longest x1 221 us: per_device(): piece_keys = lax.all_gather(keys_here, 'seq', axis=0, tiled=True)]
    another operation x2 -> x0, loops' own time: 163 us -> none  [the longest x1 99.5 us: per_device(): cache = lax.fori_loop(0, piece.shape[1] // span_len, place_one, empty_cache)]
    pallas_call x0 -> x3, Pallas kernels: none -> 117 us  [the longest x2 110 us: gather_seq(): pl.pallas_call(functools.partial(gather_kernel, nz), out_shape=jax.ShapeD...]
    reduce_sum x99 -> x0, other arithmetic: 87.6 us -> none  [the longest x65 83.4 us: span_request(): return jnp.sum((ends_incl <= page_pos).astype(jnp.int32))]
    dot_general x69 -> x1, matrix products: 79.7 us -> 5.92 us  [per_device(): jnp.dot(rows.reshape(-1, rows.shape[3]), out_weight, preferred_element_ty...]
    dynamic_slice x67 -> x0, local copies, waits for them, and re-layouts: 40 us -> none  [pick_row(): return lax.dynamic_index_in_dim(table, index, 0, keepdims=False)]
    select_n x32 -> x0, other arithmetic: 28.3 us -> none  [place_one(): return jnp.where(holds_one & (owner == chosen), written, inner)]
    all_to_all x1, waiting for transfers between devices: 0.01 us -> 21.5 us  [per_device(): lax.all_to_all(partial_rows.reshape(tp_count, tok_rows, -1), 'tp', split_...]
  transfers between devices with their start and end apart: 6 -> 2, of which waited for: 5 -> 2; matrix products, arithmetic and copies ran while one was open for 9% -> 0% of each run, Pallas kernels for 0% -> 0%
where the time goes in v1:
time: 179 us; the launch traced here: 176 us
  Pallas kernels  117 us (65%)
  waiting for transfers between devices  23.1 us (13%)
  starting transfers between devices  18.6 us (10%)
  local copies, waits for them, and re-layouts  8.21 us (5%)
  matrix products  5.92 us (3%)
  other arithmetic  3.03 us (2%)
    pallas_call x2, Pallas kernels, gather_seq(): pl.pallas_call(functools.partial(gather_kernel, nz), out_shape=jax.ShapeD...  110 us
    all_to_all x1, waiting for transfers between devices, per_device(): lax.all_to_all(partial_rows.reshape(tp_count, tok_rows, -1), 'tp', split_...  21.5 us
    ppermute x1, starting transfers between devices, per_device(): decoded = lax.ppermute(answers, 'pool', [(0, 1), (1, 0)])[None, None]  13.3 us
    unnamed x25, local copies, waits for them, and re-layouts  8.19 us
    pallas_call x1, Pallas kernels, attend(): pl.pallas_call(attend_kernel, out_shape=(jax.ShapeDtypeStruct(q.shape, BF...  6.18 us
    dot_general x1, matrix products, per_device(): jnp.dot(rows.reshape(-1, rows.shape[3]), out_weight, preferred_element_ty...  5.92 us
    all_to_all x1, starting transfers between devices, per_device(): lax.all_to_all(partial_rows.reshape(tp_count, tok_rows, -1), 'tp', split_...  5.25 us
  transfers between devices with their start and end apart: 2, of which 2 were waited for; matrix products, arithmetic and copies ran while one was open for 0% of the time, Pallas kernels for 0%

profile of v1, /device:TPU:24, one launch (start us, length us, event | category | flops | bytes accessed | tf_op | source)
XLA Modules:
  0.0 176.1 jit_solution(9807516749020361550)
XLA Ops:
  0.6 0.0 copy-start
  0.6 0.0 copy-start.3
  0.7 0.8 copy-done.3
  1.5 0.8 copy-done.4
  2.2 40.7 %shard_map.131.kv_ref = bf16[32,2,128,128]{3,2,1,0:T(8,128)(2,1)S(1)} custom-call(bf16[128,128]{1,0:T(8,128)(2,1)S(1)} %bitcast.10, bf16[128,128]{1,0:T(8,128)(2,1)S(1)} %bitcast.11), custom_call_target="tpu_custom_call" | custom-call | tf_op jit(solution)/shard_map/pallas_call | solution.py:146
  43.0 0.0 copy-start.1
  43.0 0.9 copy-done.1
  43.9 0.9 copy-done.2
  44.8 0.7 copy-done.5
  45.6 0.7 copy-done.6
  46.3 0.7 copy-done.7
  47.0 0.7 copy-done.8
  47.6 0.7 copy-done.9
  48.3 0.7 copy-done.10
  49.0 6.2 %shard_map.132 = (bf16[128,1024]{1,0:T(8,128)(2,1)S(1)}, bf16[4,1024]{1,0:T(4,128)(2,1)S(1)}) custom-call(s32[2,32]{1,0:T(2,128)S(1)} %copy-done.7, s32[2,8]{1,0:T(2,128)S(1)} %copy-done.8, s32[2,8]{1,0:T(2,128)S(1)} %copy-done.9, s32[2,8]{1,0:T(2,128)S(1)} %copy-done.10, bf16[128,1024]{1,0:T(8,128)(2,1)S(1)} %bitcast.9, ...), custom_call_target="tpu_custom_call" | custom-call | tf_op jit(solution)/shard_map/pallas_call | solution.py:310
  55.2 69.6 %shard_map.133 = bf16[32,2,64,1024]{3,2,1,0:T(8,128)(2,1)S(1)} custom-call(bf16[64,1024]{1,0:T(8,128)(2,1)S(1)} %get-tuple-element.7.first_ref, bf16[64,1024]{1,0:T(8,128)(2,1)S(1)} %get-tuple-element.6.second_ref), custom_call_target="tpu_custom_call" | custom-call | tf_op jit(solution)/shard_map/pallas_call | solution.py:146
  124.8 0.0 copy-done
  124.8 5.9 %convolution_convert_fusion = bf16[4096,384]{1,0:T(8,128)(2,1)} fusion(bf16[4096,1024]{1,0:T(8,128)(2,1)S(1)} %bitcast.8, bf16[1024,384]{1,0:T(8,128)(2,1)S(1)} %copy-done), kind=kOutput, calls=%fused_computation | convolution fusion | flops 3222798336 | bytes 12320768 | tf_op jit(solution)/shard_map/dot_general | solution.py:351
  130.7 5.2 %all-to-all-start = ((bf16[8,512,384]{2,1,0:T(8,128)(2,1)}), bf16[8,512,384]{2,1,0:T(8,128)(2,1)}, u32[]{:S(2)}, u32[]{:S(2)}) async-start(bf16[8,512,384]{2,1,0:T(8,128)(2,1)} %bitcast.12), calls=%async_computation | async-start | bytes 6291456 | tf_op jit(solution)/shard_map/all_to_all | solution.py:355
  136.0 13.3 %collective-permute-start = (bf16[4,1024]{1,0:T(4,128)(2,1)S(1)}, bf16[4,1024]{1,0:T(4,128)(2,1)S(1)}, u32[]{:S(2)}, u32[]{:S(2)}) collective-permute-start(bf16[4,1024]{1,0:T(4,128)(2,1)S(1)} %get-tuple-element.5), channel_id=1, source_target_pairs={{0,1},{1,0},{2,3},{3,2},{4,5},{5,4},{6,7},{7,6},{8,9},{9,8},{10,11... | collective-permute-start | bytes 24584 | tf_op jit(solution)/shard_map/ppermute | solution.py:347
  149.3 1.6 collective-permute-done
  150.9 21.5 %all-to-all-done = bf16[8,512,384]{2,1,0:T(8,128)(2,1)} async-done(((bf16[8,512,384]{2,1,0:T(8,128)(2,1)}), bf16[8,512,384]{2,1,0:T(8,128)(2,1)}, u32[]{:S(2)}, u32[]{:S(2)}) %all-to-all-start) | async-done | bytes 3145760 | tf_op jit(solution)/shard_map/all_to_all | solution.py:355
  172.4 3.0 %add_convert_fusion = bf16[1,512,384]{2,1,0:T(8,128)(2,1)} fusion(bf16[1,512,384]{2,1,0:T(8,128)(2,1)S(1)} %copy-done.11, bf16[8,512,384]{2,1,0:T(8,128)(2,1)} %all-to-all-done), kind=kLoop, calls=%fused_computation.1 | loop fusion | flops 3538944 | bytes 3932160 | tf_op jit(solution)/shard_map/convert_element_type | solution.py:361
  175.5 0.6 copy.15
  (11 shorter events, 0.0 us)
Async XLA Ops:
  0.6 124.2 %copy-start = (bf16[1024,384]{1,0:T(8,128)(2,1)S(1)}, bf16[1024,384]{1,0:T(8,128)(2,1)}, u32[]{:S(2)}) copy-start(bf16[1024,384]{1,0:T(8,128)(2,1)} %param.15) | copy-start | bytes 2359300
  0.6 0.8 copy-start.3
  1.5 0.8 copy-start.4
  43.0 1.0 copy-start.1
  43.9 0.9 copy-start.2
  44.8 0.7 copy-start.5
  45.6 0.7 copy-start.6
  46.3 0.7 copy-start.7
  47.0 0.7 copy-start.8
  47.6 0.7 copy-start.9
  48.3 0.7 copy-start.10
  130.7 41.7 %copy-start.11 = (bf16[1,512,384]{2,1,0:T(8,128)(2,1)S(1)}, bf16[1,512,384]{2,1,0:T(8,128)(2,1)}, u32[]{:S(2)}) copy-start(bf16[1,512,384]{2,1,0:T(8,128)(2,1)} %param.16) | copy-start | bytes 1179652
  130.7 41.7 %all-to-all-start = ((bf16[8,512,384]{2,1,0:T(8,128)(2,1)}), bf16[8,512,384]{2,1,0:T(8,128)(2,1)}, u32[]{:S(2)}, u32[]{:S(2)}) async-start(bf16[8,512,384]{2,1,0:T(8,128)(2,1)} %bitcast.12), calls=%async_computation | async-start | bytes 6291456 | tf_op jit(solution)/shard_map/all_to_all | solution.py:355
  136.0 14.9 %collective-permute-start = (bf16[4,1024]{1,0:T(4,128)(2,1)S(1)}, bf16[4,1024]{1,0:T(4,128)(2,1)S(1)}, u32[]{:S(2)}, u32[]{:S(2)}) collective-permute-start(bf16[4,1024]{1,0:T(4,128)(2,1)S(1)} %get-tuple-element.5), channel_id=1, source_target_pairs={{0,1},{1,0},{2,3},{3,2},{4,5},{5,4},{6,7},{7,6},{8,9},{9,8},{10,11... | collective-permute-start | bytes 24584 | tf_op jit(solution)/shard_map/ppermute | solution.py:347

commit v2 on v0

v2 whole, which is shorter than its diff:
```python
import math

import jax
import jax.numpy as jnp
from jax import lax
from jax.experimental import pallas as pl
from jax.experimental.pallas import tpu as pltpu
from jax.sharding import PartitionSpec as P

HD = 128
QH = 64
KVH = 8
REPEAT = QH // KVH
NX = 4
NEG_FILL = -1e30
FAR_FILL = 1e30
FACTOR = math.log2(math.e) / math.sqrt(HD)
MESH = pl.DeviceIdType.MESH
F32 = jnp.float32
BF16 = jnp.bfloat16
W_PIECES = 4


def matmul_nt(a, b):
    return lax.dot_general(a, b, (((1,), (1,)), ((), ())), preferred_element_type=F32)


def matmul_tn(a, b):
    return lax.dot_general(a, b, (((0,), (0,)), ((), ())), preferred_element_type=F32)


def remote(src, dst, send_sem, recv_sem, **target):
    return pltpu.make_async_remote_copy(
        src_ref=src,
        dst_ref=dst,
        send_sem=send_sem,
        recv_sem=recv_sem,
        device_id=target,
        device_id_type=MESH,
    )


def kernel(
    span_ref,
    counts_ref,
    tails_ref,
    dest_ref,
    dq_ref,
    dk_ref,
    dv_ref,
    k_hbm,
    v_hbm,
    q_hbm,
    w_hbm,
    res_hbm,
    out_ref,
    dec_ref,
    kv,
    q_in,
    rows_of,
    high_of,
    total_of,
    accum,
    heads_out,
    weight,
    resid,
    core_out,
    core_in,
    stash,
    y_out,
    relay_in,
    owner_in,
    x_out,
    x_in,
    dec_rows,
    new_page,
    dec_out,
    dec_in,
    local_sem,
    kz_send,
    kz_recv,
    kx_send,
    kx_recv,
    kf_send,
    kf_recv,
    wx_send,
    wx_recv,
    wf_send,
    wf_recv,
    az_send,
    az_recv,
    core_send,
    core_recv,
    y_send,
    relay_recv,
    owner_recv,
    x_send,
    x_recv,
    pool_send,
    pool_recv,
):
    me = lax.axis_index("seq")
    tp_at = lax.axis_index("tp")
    pool_at = lax.axis_index("pool")
    nz = kv.shape[0] // NX
    ny = NX
    span = kv.shape[2]
    z, x = me // NX, me % NX
    y, core = tp_at // 2, tp_at % 2
    right, left = z * NX + (x + 1) % NX, z * NX + (x + 3) % NX
    opposite = (x + 2) % NX
    sibling = tp_at + 1 - 2 * core
    part = heads_out.shape[2]
    steps = dec_ref.shape[0]
    requests = counts_ref.shape[1]

    load_k = pltpu.make_async_copy(k_hbm, kv.at[me, 0], local_sem.at[0])
    load_v = pltpu.make_async_copy(v_hbm, kv.at[me, 1], local_sem.at[1])
    load_q = pltpu.make_async_copy(q_hbm, q_in, local_sem.at[2])
    load_w = pltpu.make_async_copy(w_hbm, weight.at[x], local_sem.at[3])
    load_r = pltpu.make_async_copy(res_hbm, resid, local_sem.at[4])
    for load in (load_k, load_v, load_q, load_w, load_r):
        load.start()

    barrier = pltpu.get_barrier_semaphore()

    def greet(**target):
        pl.semaphore_signal(barrier, inc=1, device_id=target, device_id_type=MESH)

    for distance in range(1, NX):
        greet(seq=z * NX + (x + distance) % NX)
        greet(tp=((y + distance) % ny) * 2 + core)
    greet(tp=sibling)
    greet(pool=1 - pool_at)

    @pl.when(z > 0)
    def _():
        greet(seq=me - NX)

    @pl.when(z < nz - 1)
    def _():
        greet(seq=me + NX)

    load_k.wait()
    load_v.wait()
    pl.semaphore_wait(barrier, 8 + jnp.where(z > 0, 1, 0) + jnp.where(z < nz - 1, 1, 0))

    def kz_copy(zb, direction, target):
        slot = kv.at[zb * NX + x]
        return remote(slot, slot, kz_send.at[direction, zb], kz_recv.at[zb], seq=target)

    def kx_copy(zb, xb, direction, target):
        slot = kv.at[zb * NX + xb]
        return remote(
            slot, slot, kx_send.at[direction, zb], kx_recv.at[direction, zb], seq=target
        )

    def kf_copy(zb, xb, direction, target):
        slot = kv.at[zb * NX + xb, direction]
        return remote(
            slot, slot, kf_send.at[direction, zb], kf_recv.at[direction, zb], seq=target
        )

    def spread(zb):
        kx_copy(zb, x, 0, right).start()
        kx_copy(zb, x, 1, left).start()

    def relay(zb):
        kx_copy(zb, (x + 3) % NX, 0, right).wait_recv()
        kf_copy(zb, (x + 3) % NX, 0, right).start()
        kx_copy(zb, (x + 1) % NX, 1, left).wait_recv()
        kf_copy(zb, (x + 1) % NX, 1, left).start()

    height = weight.shape[1] // W_PIECES

    def w_piece(xb, piece):
        return weight.at[xb, pl.ds(piece * height, height)]

    def wx_copy(xb, piece, direction, target):
        slot = w_piece(xb, piece)
        return remote(
            slot, slot, wx_send.at[direction, piece], wx_recv.at[direction, piece], seq=target
        )

    def wf_copy(xb, n, direction, target):
        slot = w_piece(xb, direction * (W_PIECES // 2) + n)
        return remote(
            slot, slot, wf_send.at[direction, n], wf_recv.at[direction, n], seq=target
        )

    def spread_weight():
        load_w.wait()
        for n in range(W_PIECES):
            wx_copy(x, n, 0, right).start()
            wx_copy(x, (n + W_PIECES // 2) % W_PIECES, 1, left).start()

    def relay_weight(n):
        wx_copy((x + 3) % NX, n, 0, right).wait_recv()
        wf_copy((x + 3) % NX, n, 0, right).start()
        wx_copy((x + 1) % NX, n + W_PIECES // 2, 1, left).wait_recv()
        wf_copy((x + 1) % NX, n, 1, left).start()

    def finish_weight():
        for n in range(W_PIECES):
            if n >= W_PIECES // 2:
                wx_copy((x + 3) % NX, n, 0, right).wait_recv()
            else:
                wx_copy((x + 1) % NX, n, 1, left).wait_recv()
        for n in range(W_PIECES // 2):
            wf_copy(opposite, n, 0, right).wait_recv()
            wf_copy(opposite, n, 1, left).wait_recv()

    own = span_ref[pool_at, me]
    begin = jnp.int32(0)
    first = jnp.int32(0)
    dec_first, dec_count, dec_tail, dec_no, holds = (jnp.int32(0),) * 5
    for r in range(requests):
        count = counts_ref[pool_at, r]
        first = jnp.where(begin <= own, begin, first)
        match = dest_ref[pool_at, r] == me
        dec_first = jnp.where(match, begin, dec_first)
        dec_count = jnp.where(match, count, dec_count)
        dec_tail = jnp.where(match, tails_ref[pool_at, r], dec_tail)
        dec_no = jnp.where(match, r, dec_no)
        holds = jnp.where(match, 1, holds)
        begin = begin + count

    width = 2 * HD

    def attend(zb, diagonal):
        keys = kv[pl.ds(zb * NX, NX), 0].reshape(NX * span, HD)
        values = kv[pl.ds(zb * NX, NX), 1].reshape(NX * span, HD)
        pages = [span_ref[pool_at, zb * NX + j] for j in range(NX)]
        if diagonal:
            ahead = lax.broadcasted_iota(jnp.int32, (span, width), 0) - (
                lax.broadcasted_iota(jnp.int32, (span, width), 1) % span
            )
        for pair in range(REPEAT // 2):
            scores = matmul_nt(keys, rows_of[pair])
            blocks = [scores[j * span : (j + 1) * span] for j in range(NX)]
            if diagonal:
                blocks = [
                    jnp.where(
                        ahead <= jnp.where(page >= first, (own - page) * span, -2 * span),
                        block,
                        NEG_FILL,
                    )
                    for page, block in zip(pages, blocks)
                ]
                peaks = [jnp.max(block, axis=0, keepdims=True) for block in blocks]
            else:
                seen = [(page >= first) & (page < own) for page in pages]
                peaks = [
                    jnp.where(is_seen, jnp.max(block, axis=0, keepdims=True), NEG_FILL)
                    for is_seen, block in zip(seen, blocks)
                ]
            new_high = jnp.maximum(
                jnp.maximum(peaks[0], peaks[1]), jnp.maximum(peaks[2], peaks[3])
            )
            if not diagonal:
                old_high = high_of[pair, 0:1]
                new_high = jnp.maximum(new_high, old_high)
            weights = []
            sums = []
            for j, block in enumerate(blocks):
                base = new_high if diagonal else jnp.where(seen[j], new_high, FAR_FILL)
                weights.append(jnp.exp2((block - base) * FACTOR))
                sums.append(jnp.sum(weights[-1], axis=0, keepdims=True))
            total = (sums[0] + sums[1]) + (sums[2] + sums[3])
            update = matmul_tn(values, jnp.concatenate(weights, axis=0).astype(BF16))
            if not diagonal:
                fade = jnp.exp2((old_high - new_high) * FACTOR)
                total = total + total_of[pair, 0:1] * fade
                update = update + accum[pair] * fade
            high_of[pair, 0:1] = new_high
            total_of[pair, 0:1] = total
            accum[pair] = update

    lag = 1 + jnp.where((z > 0) & (z < nz - 1), 1, 0) + jnp.where((z > 1) & (z < nz - 2), 1, 0)

    load_q.wait()
    for pair in range(REPEAT // 2):
        for n in range(2):
            h = 2 * pair + n
            rows_of[pair, n * span : (n + 1) * span, :] = q_in[:, h * HD : (h + 1) * HD]

    def far_wait(zb):
        kf_copy(zb, opposite, 0, right).wait_recv()
        kf_copy(zb, opposite, 1, left).wait_recv()

    def gather_step(t, carry):
        low, high = z - t, z + t

        @pl.when((t > 0) & (low >= 0))
        def _():
            kz_copy(low, 0, me).wait_recv()

        @pl.when((low >= 0) & (z < nz - 1))
        def _():
            kz_copy(low, 0, me + NX).start()

        @pl.when((t > 0) & (high < nz))
        def _():
            kz_copy(high, 1, me).wait_recv()

        @pl.when((high < nz) & (z > 0))
        def _():
            kz_copy(high, 1, me - NX).start()

        @pl.when(low >= 0)
        def _():
            spread(low)

        @pl.when((t > 0) & (high < nz))
        def _():
            spread(high)

        past = t - lag

        @pl.when((past >= 0) & (z - past >= 0))
        def _():
            relay(z - past)

        @pl.when((past > 0) & (z + past < nz))
        def _():
            relay(z + past)

        @pl.when(t == nz)
        def _():
            spread_weight()

        ready = t - lag - 2

        @pl.when(ready == 0)
        def _():
            far_wait(z)
            attend(z, True)

        for sign in (-1, 1):
            zb = z + sign * ready

            @pl.when((ready > 0) & (zb >= 0) & (zb < nz))
            def _():
                far_wait(zb)
                attend(zb, False)

        return carry

    lax.fori_loop(0, nz + 3, gather_step, 0)

    for pair in range(REPEAT // 2):
        result = accum[pair] / total_of[pair, 0:1]
        for n in range(2):
            h = 2 * pair + n
            block = jnp.transpose(result[:, n * span : (n + 1) * span]).astype(BF16)
            for s in range(2):
                heads_out[z, s, :, h * HD : (h + 1) * HD] = block[s * part : (s + 1) * part]

    def az_copy(zb, s, direction, target):
        slot = heads_out.at[zb, s]
        return remote(slot, slot, az_send.at[direction, zb, s], az_recv.at[zb, s], seq=target)

    def z_step(t, carry):
        low, high = z - t, z + t
        for s in range(2):

            @pl.when((t > 0) & (low >= 0))
            def _():
                az_copy(low, s, 0, me).wait_recv()

            @pl.when((low >= 0) & (z < nz - 1))
            def _():
                az_copy(low, s, 0, me + NX).start()

            @pl.when((t > 0) & (high < nz))
            def _():
                az_copy(high, s, 1, me).wait_recv()

            @pl.when((high < nz) & (z > 0))
            def _():
                az_copy(high, s, 1, me - NX).start()

        return carry

    z_step(0, 0)

    queries = dq_ref[pool_at, dec_no].astype(F32)
    for h in range(REPEAT):
        dec_rows[h * steps : (h + 1) * steps, :] = queries[:, h * HD : (h + 1) * HD]
    rows = dec_rows[...].astype(BF16)
    new_page[...] = jnp.zeros_like(new_page)
    new_page[0, :steps, :] = dk_ref[pool_at, dec_no].astype(F32)
    new_page[1, :steps, :] = dv_ref[pool_at, dec_no].astype(F32)
    row_count = rows.shape[0]
    lane = lax.broadcasted_iota(jnp.int32, (row_count, span), 1)
    step_of = lax.broadcasted_iota(jnp.int32, (row_count, span), 0) % steps
    new_scores = jnp.where(
        lane <= step_of, matmul_nt(rows, new_page[0].astype(BF16)), NEG_FILL
    )
    live = (dec_count - 1) * span + dec_tail
    old_scores = []
    for zb in range(nz):
        keys = kv[zb * NX : (zb + 1) * NX, 0].reshape(NX * span, HD)
        scores = matmul_nt(rows, keys)
        for j in range(NX):
            page = span_ref[pool_at, zb * NX + j] - dec_first
            limit = jnp.where((page >= 0) & (page < dec_count), live - page * span, 0)
            old_scores.append(
                jnp.where(lane < limit, scores[:, j * span : (j + 1) * span], NEG_FILL)
            )
    peak = new_scores
    for block in old_scores:
        peak = jnp.maximum(peak, block)
    peak = jnp.max(peak, axis=1, keepdims=True)
    new_weights = jnp.exp2((new_scores - peak) * FACTOR)
    weight_sum = new_weights
    answer = jnp.dot(
        new_weights.astype(BF16), new_page[1].astype(BF16), preferred_element_type=F32
    )
    for zb in range(nz):
        row_weights = [
            jnp.exp2((old_scores[zb * NX + j] - peak) * FACTOR) for j in range(NX)
        ]
        for block in row_weights:
            weight_sum = weight_sum + block
        answer = answer + jnp.dot(
            jnp.concatenate(row_weights, axis=1).astype(BF16),
            kv[zb * NX : (zb + 1) * NX, 1].reshape(NX * span, HD),
            preferred_element_type=F32,
        )
    answer = answer / jnp.sum(weight_sum, axis=1, keepdims=True)
    dec_rows[...] = jnp.where(holds == 1, answer, 0.0)
    dec_out[...] = jnp.zeros_like(dec_out)
    for h in range(REPEAT):
        dec_out[:steps, h * HD : (h + 1) * HD] = dec_rows[
            h * steps : (h + 1) * steps, :
        ].astype(BF16)
    pool_copy = remote(dec_out, dec_in, pool_send.at[0], pool_recv.at[0], pool=1 - pool_at)
    pool_copy.start()

    def block_at(k):
        both = jnp.minimum(z, nz - 1 - z)
        near = (k + 1) // 2
        paired = jnp.where(k % 2 == 1, z - near, z + near)
        beyond = jnp.where(z < nz // 2, z + k - both, z - k + both)
        return jnp.where(k <= 2 * both, paired, beyond)

    def core_copy(slot):
        return remote(
            core_out.at[slot], core_in.at[slot], core_send.at[slot], core_recv.at[slot], tp=sibling
        )

    def place_of(item):
        zb, s = block_at(item // 2), item % 2
        owner = zb // 2
        toward = 1 - 2 * s
        rank = ((y - owner) * toward + 2 * ny) % ny
        return zb, s, owner, toward, rank, owner * 2 + s

    def project(item):
        zb, s, _, _, _, slot = place_of(item)
        block = heads_out[zb, s]
        mine = zb % 2 == core

        @pl.when(mine)
        def _():
            for c in range(NX):
                stash[slot, c] = jnp.dot(block, weight[c], preferred_element_type=F32)

        @pl.when(jnp.logical_not(mine))
        def _():
            for c in range(NX):
                core_out[slot, c] = jnp.dot(
                    block, weight[c], preferred_element_type=F32
                ).astype(BF16)
            core_copy(slot).start()

    def y_copy(slot, dst, recv_sem, target):
        return remote(y_out.at[slot], dst, y_send.at[slot], recv_sem, tp=target * 2 + core)

    def pair_sum(item):
        zb, s, owner, toward, rank, slot = place_of(item)

        @pl.when(zb % 2 == core)
        def _():
            core_copy(slot).wait_recv()
            value = stash[slot] + core_in[slot].astype(F32)

            @pl.when(rank < 2)
            def _():
                stash[slot] = value

            @pl.when(rank >= 2)
            def _():
                y_out[slot] = value.astype(BF16)

            @pl.when(rank == 2)
            def _():
                y_copy(
                    slot, relay_in.at[s], relay_recv.at[s], (owner + toward + ny) % ny
                ).start()

            @pl.when(rank == 3)
            def _():
                y_copy(slot, owner_in.at[s, 1], owner_recv.at[s, 1], owner).start()

    def relay_sum(item):
        zb, s, owner, _, rank, slot = place_of(item)

        @pl.when((zb % 2 == core) & (rank == 1))
        def _():
            y_copy(slot, relay_in.at[s], relay_recv.at[s], y).wait_recv()
            y_out[slot] = (stash[slot] + relay_in[s].astype(F32)).astype(BF16)
            y_copy(slot, owner_in.at[s, 0], owner_recv.at[s, 0], owner).start()

    def advance(t, carry):
        z_step(t, 0)

        @pl.when((t >= 1) & (t <= W_PIECES // 2))
        def _():
            relay_weight(t - 1)

        return carry

    lax.fori_loop(1, 5, advance, 0)
    finish_weight()

    def item_step(item, carry):
        k = item // 2

        @pl.when((item % 2 == 0) & ((k == 2) | (k == 4) | (k == 7)))
        def _():
            z_step(jnp.where(k == 2, 5, jnp.where(k == 4, 6, 7)), 0)

        @pl.when(item < 2 * nz)
        def _():
            project(item)

        @pl.when((item >= 2) & (item < 2 * nz + 2))
        def _():
            pair_sum(item - 2)

        @pl.when((item >= 5) & (item < 2 * nz + 5))
        def _():
            relay_sum(item - 5)

        return carry

    lax.fori_loop(0, 2 * nz + 5, item_step, 0)

    def x_copy(s, distance):
        target = (x + distance) % NX
        return remote(
            x_out.at[s, target],
            x_in.at[x, s],
            x_send.at[s, distance],
            x_recv.at[s, distance],
            seq=z * NX + target,
        )

    load_r.wait()

    def finish(source, s, value):
        row = source * 2 * part + s * part
        out_ref[pl.ds(row, part), :] = (
            value.astype(F32) + resid[pl.ds(row, part), :].astype(F32)
        ).astype(BF16)

    for s in range(2):
        slot = y * 2 + s
        for n in range(2):
            y_copy(slot, owner_in.at[s, n], owner_recv.at[s, n], y).wait_recv()
        total = stash[slot] + owner_in[s, 0].astype(F32) + owner_in[s, 1].astype(F32)
        x_out[s] = total.astype(BF16)
        for distance in range(1, NX):
            x_copy(s, distance).start()
    for s in range(2):
        finish(x, s, x_out[s, x])
    for s in range(2):
        for distance in range(1, NX):
            source = (x + NX - distance) % NX
            remote(
                x_out.at[s, x],
                x_in.at[source, s],
                x_send.at[s, distance],
                x_recv.at[s, distance],
                seq=me,
            ).wait_recv()
            finish(source, s, x_in[source, s])

    pool_copy.wait()
    dec_ref[...] = dec_in[:steps, :]

    def drain(zb, carry):
        @pl.when((zb <= z) & (z < nz - 1))
        def _():
            kz_copy(zb, 0, me).wait_send()
            for s in range(2):
                az_copy(zb, s, 0, me).wait_send()

        @pl.when((zb >= z) & (z > 0))
        def _():
            kz_copy(zb, 1, me).wait_send()
            for s in range(2):
                az_copy(zb, s, 1, me).wait_send()

        kx_copy(zb, x, 0, right).wait_send()
        kx_copy(zb, x, 1, left).wait_send()
        kf_copy(zb, opposite, 0, right).wait_send()
        kf_copy(zb, opposite, 1, left).wait_send()

        for s in range(2):
            slot = (zb // 2) * 2 + s

            @pl.when(zb % 2 != core)
            def _():
                core_copy(slot).wait_send()

            @pl.when((zb % 2 == core) & (zb // 2 != y))
            def _():
                y_copy(slot, relay_in.at[s], relay_recv.at[s], y).wait_send()

        return carry

    lax.fori_loop(0, nz, drain, 0)
    for n in range(W_PIECES):
        wx_copy(x, n, 0, right).wait_send()
        wx_copy(x, n, 1, left).wait_send()
    for n in range(W_PIECES // 2):
        wf_copy(opposite, n, 0, right).wait_send()
        wf_copy(opposite, n, 1, left).wait_send()
    for s in range(2):
        for distance in range(1, NX):
            x_copy(s, distance).wait_send()


def per_device(
    q_pre,
    k_pre,
    v_pre,
    out_weight,
    residual,
    span_ids,
    page_counts,
    tail_rows,
    dest_group,
    dec_q,
    dec_k,
    dec_v,
):
    count = lax.axis_size("seq")
    nz = count // NX
    span, features = q_pre.shape[1:]
    depth, columns = out_weight.shape
    steps = dec_q.shape[2]
    part = span // 2
    pairs = REPEAT // 2
    dma = pltpu.SemaphoreType.DMA
    vmem, smem, hbm = (
        pl.BlockSpec(memory_space=space) for space in (pltpu.VMEM, pltpu.SMEM, pltpu.HBM)
    )
    tile = (NX, part, columns)
    mixed, decoded = pl.pallas_call(
        kernel,
        out_shape=(
            jax.ShapeDtypeStruct(residual.shape[1:], BF16),
            jax.ShapeDtypeStruct((steps, features), BF16),
        ),
        in_specs=[smem] * 4 + [vmem] * 3 + [hbm] * 5,
        out_specs=(vmem, vmem),
        scratch_shapes=[
            pltpu.VMEM((count, 2, span, HD), BF16),
            pltpu.VMEM((span, features), BF16),
            pltpu.VMEM((pairs, 2 * span, HD), BF16),
            pltpu.VMEM((pairs, 8, 2 * span), F32),
            pltpu.VMEM((pairs, 8, 2 * span), F32),
            pltpu.VMEM((pairs, HD, 2 * span), F32),
            pltpu.VMEM((nz, 2, part, features), BF16),
            pltpu.VMEM((NX, depth, columns), BF16),
            pltpu.VMEM(residual.shape[1:], BF16),
            pltpu.VMEM((nz,) + tile, BF16),
            pltpu.VMEM((nz,) + tile, BF16),
            pltpu.VMEM((nz,) + tile, F32),
            pltpu.VMEM((nz,) + tile, BF16),
            pltpu.VMEM((2,) + tile, BF16),
            pltpu.VMEM((2, 2) + tile, BF16),
            pltpu.VMEM((2,) + tile, BF16),
            pltpu.VMEM((NX, 2, part, columns), BF16),
            pltpu.VMEM((steps * REPEAT, HD), F32),
            pltpu.VMEM((2, span, HD), F32),
            pltpu.VMEM((16, features), BF16),
            pltpu.VMEM((16, features), BF16),
            dma((5,)),
            dma((2, nz)),
            dma((nz,)),
            dma((2, nz)),
            dma((2, nz)),
            dma((2, nz)),
            dma((2, nz)),
            dma((2, W_PIECES)),
            dma((2, W_PIECES)),
            dma((2, W_PIECES // 2)),
            dma((2, W_PIECES // 2)),
            dma((2, nz, 2)),
            dma((nz, 2)),
            dma((nz,)),
            dma((nz,)),
            dma((nz,)),
            dma((2,)),
            dma((2, 2)),
            dma((2, NX)),
            dma((2, NX)),
            dma((1,)),
            dma((1,)),
        ],
        compiler_params=pltpu.CompilerParams(
            collective_id=0, has_side_effects=True, vmem_limit_bytes=48 << 20
        ),
    )(
        span_ids,
        page_counts,
        tail_rows,
        dest_group,
        dec_q,
        dec_k,
        dec_v,
        k_pre[0],
        v_pre[0],
        q_pre[0],
        out_weight,
        residual[0],
    )
    return (mixed[None], decoded[None, None])


def solution(mesh):
    placed = (
        P("pool", "seq", "tp"),
        P("pool", "seq", "tp"),
        P("pool", "seq", "tp"),
        P("tp", "seq"),
        P("pool", "tp", "seq"),
        P(),
        P(),
        P(),
        P(),
        P(None, None, None, "tp"),
        P(None, None, None, "tp"),
        P(None, None, None, "tp"),
    )
    return jax.shard_map(
        per_device,
        mesh=mesh,
        in_specs=placed,
        out_specs=(P("pool", "tp", "seq"), P("pool", "seq", None, "tp")),
        check_vma=False,
    )
```

time: 1250 us -> 138 us (0.11)
  waiting for transfers between devices: 799 us -> 0 us
  loops' own time: 163 us -> 0 us
  Pallas kernels: 0 us -> 128 us
  other arithmetic: 126 us -> 0 us
  matrix products: 79.7 us -> 0 us
  local copies, waits for them, and re-layouts: 46.5 us -> 8.97 us
  between operations: 17.4 us -> 0.69 us
    all_gather x4 -> x0, waiting for transfers between devices: 789 us -> none  [the longest x1 221 us: per_device(): piece_keys = lax.all_gather(keys_here, 'seq', axis=0, tiled=True)]
    another operation x2 -> x0, loops' own time: 163 us -> none  [the longest x1 99.5 us: per_device(): cache = lax.fori_loop(0, piece.shape[1] // span_len, place_one, empty_cache)]
    pallas_call x0 -> x1, Pallas kernels: none -> 128 us  [per_device(): pl.pallas_call(kernel, out_shape=(jax.ShapeDtypeStruct(residual.shape[1:]...]
    reduce_sum x99 -> x0, other arithmetic: 87.6 us -> none  [the longest x65 83.4 us: span_request(): return jnp.sum((ends_incl <= page_pos).astype(jnp.int32))]
    dot_general x69 -> x0, matrix products: 79.7 us -> none  [the longest x32 35.2 us: attend_shard(): jnp.einsum('qgrk,kgd->qgrd', weights.astype(jnp.bfloat16), shard_values.r...]
    dynamic_slice x67 -> x0, local copies, waits for them, and re-layouts: 40 us -> none  [pick_row(): return lax.dynamic_index_in_dim(table, index, 0, keepdims=False)]
    select_n x32 -> x0, other arithmetic: 28.3 us -> none  [place_one(): return jnp.where(holds_one & (owner == chosen), written, inner)]
  transfers between devices with their start and end apart: 6 -> 0, of which waited for: 5 -> 0; matrix products, arithmetic and copies ran while one was open for 9% -> 0% of each run, Pallas kernels for 0% -> 0%
where the time goes in v2:
time: 138 us
  Pallas kernels  128 us (93%)
  local copies, waits for them, and re-layouts  8.97 us (7%)
    pallas_call x1, Pallas kernels, per_device(): pl.pallas_call(kernel, out_shape=(jax.ShapeDtypeStruct(residual.shape[1:]...  128 us
    unnamed x26, local copies, waits for them, and re-layouts  8.97 us

profile of v2, /device:TPU:24, one launch (start us, length us, event | category | flops | bytes accessed | tf_op | source)
XLA Modules:
  0.0 137.6 jit_solution(4382534674677307003)
XLA Ops:
  0.6 0.0 copy-start.11
  0.6 0.0 copy-start.9
  0.7 0.0 copy-start.10
  0.7 0.0 copy-start.8
  0.7 0.6 copy-done.11
  1.3 0.0 copy-done.9
  1.3 0.0 copy-done.10
  1.3 0.0 copy-done.8
  1.4 0.0 copy-start
  1.4 1.1 copy-done
  2.5 0.0 copy-start.1
  2.5 1.0 copy-done.1
  3.5 0.0 copy-start.2
  3.5 0.9 copy-done.2
  4.4 0.0 copy-start.3
  4.4 0.9 copy-done.3
  5.3 0.0 copy-start.4
  5.3 0.8 copy-done.4
  6.1 0.8 copy-done.5
  6.9 0.7 copy-done.6
  7.6 0.7 copy-done.7
  8.3 128.0 %shard_map.131 = (bf16[512,384]{1,0:T(8,128)(2,1)S(1)}, bf16[4,1024]{1,0:T(4,128)(2,1)S(1)}) custom-call(s32[2,32]{1,0:T(2,128)S(1)} %copy-done.8, s32[2,8]{1,0:T(2,128)S(1)} %copy-done.9, s32[2,8]{1,0:T(2,128)S(1)} %copy-done.10, s32[2,8]{1,0:T(2,128)S(1)} %copy-done.11, bf16[2,8,4,1024]{3,2,1,0:T(4,128)(2,1)S(1)} %copy-done.3, ...), custom_call_target="tpu_custom_call" | custom-call | tf_op jit(solution)/shard_map/pallas_call | solution.py:663
  136.3 0.7 copy.16
  137.0 0.6 copy.17
  (3 shorter events, 0.0 us)
Async XLA Ops:
  0.6 0.7 copy-start.11
  0.6 0.7 copy-start.9
  0.7 0.7 copy-start.10
  0.7 0.7 copy-start.8
  1.4 1.1 copy-start
  2.5 1.0 copy-start.1
  3.5 0.9 copy-start.2
  4.4 0.9 copy-start.3
  5.3 0.8 copy-start.4
  6.1 0.8 copy-start.5
  6.9 0.7 copy-start.6
  7.6 0.7 copy-start.7

commit v3 on v2

--- a/solution.py
+++ b/solution.py
@@ -19,6 +19,30 @@
 F32 = jnp.float32
 BF16 = jnp.bfloat16
 W_PIECES = 4
+W_START = 8
+W_RELAY = 1
+RELAY_LAG = 8
+OWNER_LAG = 12
+
+
+def unit(block, *turns):
+    return [block * 4 + turn for turn in turns]
+
+
+SEGMENTS = [
+    unit(0, 0),
+    unit(1, 0),
+    unit(2, 0),
+    unit(3, 0) + unit(0, 1, 2) + unit(1, 1, 2),
+    unit(4, 0) + unit(2, 1, 2) + unit(3, 1, 2) + unit(4, 1, 2),
+    unit(5, 0, 1, 2) + unit(0, 3) + unit(1, 3) + unit(2, 3) + unit(3, 3) + unit(4, 3),
+    unit(5, 3) + unit(6, 3, 1, 2, 0),
+    unit(7, 3, 1, 2, 0),
+]
+UNITS = sum(SEGMENTS, [])
+STEP_AT = [sum(len(segment) for segment in SEGMENTS[:t]) for t in range(len(SEGMENTS))]
+NEAR_AT = UNITS.index(1)
+FAR_AT = UNITS.index(3)
 
 
 def matmul_nt(a, b):
@@ -45,9 +69,9 @@
     counts_ref,
     tails_ref,
     dest_ref,
-    dq_ref,
-    dk_ref,
-    dv_ref,
+    dq_hbm,
+    dk_hbm,
+    dv_hbm,
     k_hbm,
     v_hbm,
     q_hbm,
@@ -55,6 +79,9 @@
     res_hbm,
     out_ref,
     dec_ref,
+    dq_ref,
+    dk_ref,
+    dv_ref,
     kv,
     q_in,
     rows_of,
@@ -119,7 +146,11 @@
     load_q = pltpu.make_async_copy(q_hbm, q_in, local_sem.at[2])
     load_w = pltpu.make_async_copy(w_hbm, weight.at[x], local_sem.at[3])
     load_r = pltpu.make_async_copy(res_hbm, resid, local_sem.at[4])
-    for load in (load_k, load_v, load_q, load_w, load_r):
+    load_dec = [
+        pltpu.make_async_copy(src, dst, local_sem.at[5 + n])
+        for n, (src, dst) in enumerate(((dq_hbm, dq_ref), (dk_hbm, dk_ref), (dv_hbm, dv_ref)))
+    ]
+    for load in (load_k, load_v, load_q, load_w, load_r, *load_dec):
         load.start()
 
     barrier = pltpu.get_barrier_semaphore()
@@ -145,9 +176,11 @@
     load_v.wait()
     pl.semaphore_wait(barrier, 8 + jnp.where(z > 0, 1, 0) + jnp.where(z < nz - 1, 1, 0))
 
-    def kz_copy(zb, direction, target):
-        slot = kv.at[zb * NX + x]
-        return remote(slot, slot, kz_send.at[direction, zb], kz_recv.at[zb], seq=target)
+    def kz_copy(zb, which, direction, target):
+        slot = kv.at[zb * NX + x, which]
+        return remote(
+            slot, slot, kz_send.at[direction, zb, which], kz_recv.at[zb, which], seq=target
+        )
 
     def kx_copy(zb, xb, direction, target):
         slot = kv.at[zb * NX + xb]
@@ -200,12 +233,12 @@
         wx_copy((x + 1) % NX, n + W_PIECES // 2, 1, left).wait_recv()
         wf_copy((x + 1) % NX, n, 1, left).start()
 
-    def finish_weight():
-        for n in range(W_PIECES):
-            if n >= W_PIECES // 2:
-                wx_copy((x + 3) % NX, n, 0, right).wait_recv()
-            else:
-                wx_copy((x + 1) % NX, n, 1, left).wait_recv()
+    def finish_near():
+        for n in range(W_PIECES // 2):
+            wx_copy((x + 3) % NX, n + W_PIECES // 2, 0, right).wait_recv()
+            wx_copy((x + 1) % NX, n, 1, left).wait_recv()
+
+    def finish_far():
         for n in range(W_PIECES // 2):
             wf_copy(opposite, n, 0, right).wait_recv()
             wf_copy(opposite, n, 1, left).wait_recv()
@@ -291,28 +324,30 @@
     def gather_step(t, carry):
         low, high = z - t, z + t
 
-        @pl.when((t > 0) & (low >= 0))
-        def _():
-            kz_copy(low, 0, me).wait_recv()
-
-        @pl.when((low >= 0) & (z < nz - 1))
-        def _():
-            kz_copy(low, 0, me + NX).start()
+        for which in range(2):
+
+            @pl.when((t > 0) & (low >= 0))
+            def _():
+                kz_copy(low, which, 0, me).wait_recv()
+
+            @pl.when((low >= 0) & (z < nz - 1))
+            def _():
+                kz_copy(low, which, 0, me + NX).start()
+
+            @pl.when((t > 0) & (high < nz))
+            def _():
+                kz_copy(high, which, 1, me).wait_recv()
+
+            @pl.when((high < nz) & (z > 0))
+            def _():
+                kz_copy(high, which, 1, me - NX).start()
+
+        @pl.when(low >= 0)
+        def _():
+            spread(low)
 
         @pl.when((t > 0) & (high < nz))
         def _():
-            kz_copy(high, 1, me).wait_recv()
-
-        @pl.when((high < nz) & (z > 0))
-        def _():
-            kz_copy(high, 1, me - NX).start()
-
-        @pl.when(low >= 0)
-        def _():
-            spread(low)
-
-        @pl.when((t > 0) & (high < nz))
-        def _():
             spread(high)
 
         past = t - lag
@@ -325,7 +360,7 @@
         def _():
             relay(z + past)
 
-        @pl.when(t == nz)
+        @pl.when(t == W_START)
         def _():
             spread_weight()
 
@@ -384,6 +419,8 @@
 
     z_step(0, 0)
 
+    for load in load_dec:
+        load.wait()
     queries = dq_ref[pool_at, dec_no].astype(F32)
     for h in range(REPEAT):
         dec_rows[h * steps : (h + 1) * steps, :] = queries[:, h * HD : (h + 1) * HD]
@@ -438,50 +475,53 @@
     pool_copy = remote(dec_out, dec_in, pool_send.at[0], pool_recv.at[0], pool=1 - pool_at)
     pool_copy.start()
 
-    def block_at(k):
-        both = jnp.minimum(z, nz - 1 - z)
+    edge = jnp.minimum(z, nz - 1 - z)
+
+    def look_up(table, index):
+        value = jnp.int32(table[-1])
+        for n in reversed(range(len(table) - 1)):
+            value = jnp.where(index <= n, table[n], value)
+        return value
+
+    def place_of(unit):
+        code = look_up(UNITS, unit)
+        k, turn = code // 4, code % 4
         near = (k + 1) // 2
         paired = jnp.where(k % 2 == 1, z - near, z + near)
-        beyond = jnp.where(z < nz // 2, z + k - both, z - k + both)
-        return jnp.where(k <= 2 * both, paired, beyond)
+        beyond = jnp.where(z < nz // 2, z + k - edge, z - k + edge)
+        zb = jnp.where(k <= 2 * edge, paired, beyond)
+        quarter = (x + jnp.where(turn == 1, 3, jnp.where(turn == 2, 1, jnp.where(turn == 3, 2, 0)))) % NX
+        owner = zb // 2
+        toward = 1 - 2 * (quarter % 2)
+        rank = ((y - owner) * toward + 2 * ny) % ny
+        return zb % 2 == core, zb, quarter, owner, toward, rank, owner * NX + quarter
 
     def core_copy(slot):
         return remote(
             core_out.at[slot], core_in.at[slot], core_send.at[slot], core_recv.at[slot], tp=sibling
         )
 
-    def place_of(item):
-        zb, s = block_at(item // 2), item % 2
-        owner = zb // 2
-        toward = 1 - 2 * s
-        rank = ((y - owner) * toward + 2 * ny) % ny
-        return zb, s, owner, toward, rank, owner * 2 + s
-
-    def project(item):
-        zb, s, _, _, _, slot = place_of(item)
-        block = heads_out[zb, s]
-        mine = zb % 2 == core
+    def project(unit):
+        mine, zb, quarter, _, _, _, slot = place_of(unit)
+        block = heads_out[zb].reshape(span, heads_out.shape[3])
+        product = jnp.dot(block, weight[quarter], preferred_element_type=F32)
 
         @pl.when(mine)
         def _():
-            for c in range(NX):
-                stash[slot, c] = jnp.dot(block, weight[c], preferred_element_type=F32)
+            stash[slot] = product
 
         @pl.when(jnp.logical_not(mine))
         def _():
-            for c in range(NX):
-                core_out[slot, c] = jnp.dot(
-                    block, weight[c], preferred_element_type=F32
-                ).astype(BF16)
+            core_out[slot] = product.astype(BF16)
             core_copy(slot).start()
 
     def y_copy(slot, dst, recv_sem, target):
         return remote(y_out.at[slot], dst, y_send.at[slot], recv_sem, tp=target * 2 + core)
 
-    def pair_sum(item):
-        zb, s, owner, toward, rank, slot = place_of(item)
-
-        @pl.when(zb % 2 == core)
+    def pair_sum(unit, carry):
+        mine, _, quarter, owner, toward, rank, slot = place_of(unit)
+
+        @pl.when(mine)
         def _():
             core_copy(slot).wait_recv()
             value = stash[slot] + core_in[slot].astype(F32)
@@ -497,96 +537,132 @@
             @pl.when(rank == 2)
             def _():
                 y_copy(
-                    slot, relay_in.at[s], relay_recv.at[s], (owner + toward + ny) % ny
+                    slot, relay_in.at[quarter], relay_recv.at[quarter], (owner + toward + ny) % ny
                 ).start()
 
             @pl.when(rank == 3)
             def _():
-                y_copy(slot, owner_in.at[s, 1], owner_recv.at[s, 1], owner).start()
-
-    def relay_sum(item):
-        zb, s, owner, _, rank, slot = place_of(item)
-
-        @pl.when((zb % 2 == core) & (rank == 1))
-        def _():
-            y_copy(slot, relay_in.at[s], relay_recv.at[s], y).wait_recv()
-            y_out[slot] = (stash[slot] + relay_in[s].astype(F32)).astype(BF16)
-            y_copy(slot, owner_in.at[s, 0], owner_recv.at[s, 0], owner).start()
+                y_copy(
+                    slot, owner_in.at[quarter, 1], owner_recv.at[quarter, 1], owner
+                ).start()
+
+        return carry
+
+    def relay_sum(unit, carry):
+        mine, _, quarter, owner, _, rank, slot = place_of(unit)
+
+        @pl.when(mine & (rank == 1))
+        def _():
+            y_copy(slot, relay_in.at[quarter], relay_recv.at[quarter], y).wait_recv()
+            y_out[slot] = (stash[slot] + relay_in[quarter].astype(F32)).astype(BF16)
+            y_copy(slot, owner_in.at[quarter, 0], owner_recv.at[quarter, 0], owner).start()
+
+        return carry
+
+    def x_copy(quarter, source, target):
+        distance = (target + NX - source) % NX
+        return remote(
+            x_out.at[quarter],
+            x_in.at[source],
+            x_send.at[distance],
+            x_recv.at[distance],
+            seq=z * NX + target,
+        )
+
+    def finish(source, value):
+        row = pl.ds(source * span, span)
+        out_ref[row, :] = (value.astype(F32) + resid[row, :].astype(F32)).astype(BF16)
+
+    def owner_sum(unit, carry):
+        mine, _, quarter, _, _, rank, slot = place_of(unit)
+
+        @pl.when(mine & (rank == 0))
+        def _():
+            for n in range(2):
+                y_copy(slot, owner_in.at[quarter, n], owner_recv.at[quarter, n], y).wait_recv()
+            total = (
+                stash[slot]
+                + owner_in[quarter, 0].astype(F32)
+                + owner_in[quarter, 1].astype(F32)
+            )
+
+            @pl.when(quarter == x)
+            def _():
+                finish(x, total)
+
+            @pl.when(quarter != x)
+            def _():
+                x_out[quarter] = total.astype(BF16)
+                x_copy(quarter, x, quarter).start()
+
+        return carry
+
+    count = len(UNITS)
+
+    def clipped(value):
+        return jnp.clip(value, 0, count)
+
+    def flushing(unit):
+        return (unit >= count) | ((edge == 0) & ((unit == STEP_AT[6]) | (unit == STEP_AT[7])))
+
+    def pairs_by(unit):
+        return clipped(jnp.where(unit >= count, unit, unit - 1 + jnp.where(flushing(unit), 1, 0)))
+
+    def relays_by(unit):
+        late = jnp.where(unit >= STEP_AT[7], count - 4 + unit - count, unit - RELAY_LAG)
+        return clipped(late)
+
+    def owners_by(unit):
+        late = jnp.where(unit > count, count - 5 + unit - count, unit - OWNER_LAG)
+        return clipped(late)
+
+    def steps_by(unit):
+        done = jnp.int32(0)
+        for t in range(1, nz):
+            at = jnp.int32(STEP_AT[t])
+            if t == 5:
+                at = at - jnp.where((edge == 1) | (edge == 2), 2, 0)
+            if t == 6:
+                at = at - jnp.where(edge == 1, 2, 0)
+            done = done + jnp.where(unit >= at, 1, 0)
+        return done
 
     def advance(t, carry):
         z_step(t, 0)
 
-        @pl.when((t >= 1) & (t <= W_PIECES // 2))
-        def _():
-            relay_weight(t - 1)
+        @pl.when((t >= W_RELAY) & (t < W_RELAY + W_PIECES // 2))
+        def _():
+            relay_weight(t - W_RELAY)
 
         return carry
 
-    lax.fori_loop(1, 5, advance, 0)
-    finish_weight()
-
-    def item_step(item, carry):
-        k = item // 2
-
-        @pl.when((item % 2 == 0) & ((k == 2) | (k == 4) | (k == 7)))
-        def _():
-            z_step(jnp.where(k == 2, 5, jnp.where(k == 4, 6, 7)), 0)
-
-        @pl.when(item < 2 * nz)
-        def _():
-            project(item)
-
-        @pl.when((item >= 2) & (item < 2 * nz + 2))
-        def _():
-            pair_sum(item - 2)
-
-        @pl.when((item >= 5) & (item < 2 * nz + 5))
-        def _():
-            relay_sum(item - 5)
+    def unit_step(unit, carry):
+        lax.fori_loop(pairs_by(unit - 1), pairs_by(unit), pair_sum, 0)
+        lax.fori_loop(relays_by(unit - 1), relays_by(unit), relay_sum, 0)
+        lax.fori_loop(owners_by(unit - 1), owners_by(unit), owner_sum, 0)
+        lax.fori_loop(steps_by(unit - 1) + 1, steps_by(unit) + 1, advance, 0)
+
+        @pl.when(unit == NEAR_AT)
+        def _():
+            finish_near()
+
+        @pl.when(unit == FAR_AT)
+        def _():
+            finish_far()
+
+        @pl.when(unit < count)
+        def _():
+            project(unit)
 
         return carry
 
-    lax.fori_loop(0, 2 * nz + 5, item_step, 0)
-
-    def x_copy(s, distance):
-        target = (x + distance) % NX
-        return remote(
-            x_out.at[s, target],
-            x_in.at[x, s],
-            x_send.at[s, distance],
-            x_recv.at[s, distance],
-            seq=z * NX + target,
-        )
-
     load_r.wait()
-
-    def finish(source, s, value):
-        row = source * 2 * part + s * part
-        out_ref[pl.ds(row, part), :] = (
-            value.astype(F32) + resid[pl.ds(row, part), :].astype(F32)
-        ).astype(BF16)
-
-    for s in range(2):
-        slot = y * 2 + s
-        for n in range(2):
-            y_copy(slot, owner_in.at[s, n], owner_recv.at[s, n], y).wait_recv()
-        total = stash[slot] + owner_in[s, 0].astype(F32) + owner_in[s, 1].astype(F32)
-        x_out[s] = total.astype(BF16)
-        for distance in range(1, NX):
-            x_copy(s, distance).start()
-    for s in range(2):
-        finish(x, s, x_out[s, x])
-    for s in range(2):
-        for distance in range(1, NX):
-            source = (x + NX - distance) % NX
-            remote(
-                x_out.at[s, x],
-                x_in.at[source, s],
-                x_send.at[s, distance],
-                x_recv.at[s, distance],
-                seq=me,
-            ).wait_recv()
-            finish(source, s, x_in[source, s])
+    lax.fori_loop(0, count + 6, unit_step, 0)
+
+    for distance in range(1, NX):
+        source = (x + NX - distance) % NX
+        x_copy(x, source, x).wait_recv()
+        finish(source, x_in[source])
 
     pool_copy.wait()
     dec_ref[...] = dec_in[:steps, :]
@@ -594,14 +670,14 @@
     def drain(zb, carry):
         @pl.when((zb <= z) & (z < nz - 1))
         def _():
-            kz_copy(zb, 0, me).wait_send()
             for s in range(2):
+                kz_copy(zb, s, 0, me).wait_send()
                 az_copy(zb, s, 0, me).wait_send()
 
         @pl.when((zb >= z) & (z > 0))
         def _():
-            kz_copy(zb, 1, me).wait_send()
             for s in range(2):
+                kz_copy(zb, s, 1, me).wait_send()
                 az_copy(zb, s, 1, me).wait_send()
 
         kx_copy(zb, x, 0, right).wait_send()
@@ -609,8 +685,8 @@
         kf_copy(zb, opposite, 0, right).wait_send()
         kf_copy(zb, opposite, 1, left).wait_send()
 
-        for s in range(2):
-            slot = (zb // 2) * 2 + s
+        for quarter in range(NX):
+            slot = (zb // 2) * NX + quarter
 
             @pl.when(zb % 2 != core)
             def _():
@@ -618,7 +694,7 @@
 
             @pl.when((zb % 2 == core) & (zb // 2 != y))
             def _():
-                y_copy(slot, relay_in.at[s], relay_recv.at[s], y).wait_send()
+                y_copy(slot, relay_in.at[quarter], relay_recv.at[quarter], y).wait_send()
 
         return carry
 
@@ -629,9 +705,9 @@
     for n in range(W_PIECES // 2):
         wf_copy(opposite, n, 0, right).wait_send()
         wf_copy(opposite, n, 1, left).wait_send()
-    for s in range(2):
-        for distance in range(1, NX):
-            x_copy(s, distance).wait_send()
+    for distance in range(1, NX):
+        target = (x + distance) % NX
+        x_copy(target, x, target).wait_send()
 
 
 def per_device(
@@ -654,21 +730,25 @@
     depth, columns = out_weight.shape
     steps = dec_q.shape[2]
     part = span // 2
+    slots = nz // 2 * NX
     pairs = REPEAT // 2
     dma = pltpu.SemaphoreType.DMA
     vmem, smem, hbm = (
         pl.BlockSpec(memory_space=space) for space in (pltpu.VMEM, pltpu.SMEM, pltpu.HBM)
     )
-    tile = (NX, part, columns)
+    tile = (span, columns)
     mixed, decoded = pl.pallas_call(
         kernel,
         out_shape=(
             jax.ShapeDtypeStruct(residual.shape[1:], BF16),
             jax.ShapeDtypeStruct((steps, features), BF16),
         ),
-        in_specs=[smem] * 4 + [vmem] * 3 + [hbm] * 5,
+        in_specs=[smem] * 4 + [hbm] * 8,
         out_specs=(vmem, vmem),
         scratch_shapes=[
+            pltpu.VMEM(dec_q.shape, BF16),
+            pltpu.VMEM(dec_k.shape, BF16),
+            pltpu.VMEM(dec_v.shape, BF16),
             pltpu.VMEM((count, 2, span, HD), BF16),
             pltpu.VMEM((span, features), BF16),
             pltpu.VMEM((pairs, 2 * span, HD), BF16),
@@ -678,21 +758,21 @@
             pltpu.VMEM((nz, 2, part, features), BF16),
             pltpu.VMEM((NX, depth, columns), BF16),
             pltpu.VMEM(residual.shape[1:], BF16),
-            pltpu.VMEM((nz,) + tile, BF16),
-            pltpu.VMEM((nz,) + tile, BF16),
-            pltpu.VMEM((nz,) + tile, F32),
-            pltpu.VMEM((nz,) + tile, BF16),
-            pltpu.VMEM((2,) + tile, BF16),
-            pltpu.VMEM((2, 2) + tile, BF16),
-            pltpu.VMEM((2,) + tile, BF16),
-            pltpu.VMEM((NX, 2, part, columns), BF16),
+            pltpu.VMEM((slots,) + tile, BF16),
+            pltpu.VMEM((slots,) + tile, BF16),
+            pltpu.VMEM((slots,) + tile, F32),
+            pltpu.VMEM((slots,) + tile, BF16),
+            pltpu.VMEM((NX,) + tile, BF16),
+            pltpu.VMEM((NX, 2) + tile, BF16),
+            pltpu.VMEM((NX,) + tile, BF16),
+            pltpu.VMEM((NX,) + tile, BF16),
             pltpu.VMEM((steps * REPEAT, HD), F32),
             pltpu.VMEM((2, span, HD), F32),
             pltpu.VMEM((16, features), BF16),
             pltpu.VMEM((16, features), BF16),
-            dma((5,)),
-            dma((2, nz)),
-            dma((nz,)),
+            dma((8,)),
+            dma((2, nz, 2)),
+            dma((nz, 2)),
             dma((2, nz)),
             dma((2, nz)),
             dma((2, nz)),
@@ -703,18 +783,18 @@
             dma((2, W_PIECES // 2)),
             dma((2, nz, 2)),
             dma((nz, 2)),
-            dma((nz,)),
-            dma((nz,)),
-            dma((nz,)),
-            dma((2,)),
-            dma((2, 2)),
-            dma((2, NX)),
-            dma((2, NX)),
+            dma((slots,)),
+            dma((slots,)),
+            dma((slots,)),
+            dma((NX,)),
+            dma((NX, 2)),
+            dma((NX,)),
+            dma((NX,)),
             dma((1,)),
             dma((1,)),
         ],
         compiler_params=pltpu.CompilerParams(
-            collective_id=0, has_side_effects=True, vmem_limit_bytes=48 << 20
+            collective_id=0, has_side_effects=True, vmem_limit_bytes=60 << 20
         ),
     )(
         span_ids,

time: 138 us -> 117 us (0.85)
  the two profiles are of different devices: /device:TPU:24 before, /device:TPU:27 now
where the time goes in v3:
time: 117 us; the launch traced here: 116 us
  Pallas kernels  113 us (97%)
  local copies, waits for them, and re-layouts  2.39 us (2%)
    pallas_call x1, Pallas kernels, per_device(): pl.pallas_call(kernel, out_shape=(jax.ShapeDtypeStruct(residual.shape[1:]...  113 us
    unnamed x4, local copies, waits for them, and re-layouts  2.39 us

profile of v3, /device:TPU:27, one launch (start us, length us, event | category | flops | bytes accessed | tf_op | source)
XLA Modules:
  0.0 116.4 jit_solution(2663017282537241359)
XLA Ops:
  0.6 113.4 %shard_map.131 = (bf16[512,384]{1,0:T(8,128)(2,1)}, bf16[4,1024]{1,0:T(4,128)(2,1)}) custom-call(s32[2,32]{1,0:T(2,128)} %span_ref.1, s32[2,8]{1,0:T(2,128)} %counts_ref.1, s32[2,8]{1,0:T(2,128)} %tails_ref.1, s32[2,8]{1,0:T(2,128)} %dest_ref.1, bf16[2,8,4,1024]{3,2,1,0:T(4,128)(2,1)} %dq_hbm.1, bf16[2,8,4,128]{3,2,1,0:T(4,128)(2,1)} %dk_hbm.1, ...), custom_call_target="tpu_custom_call" | custom-call | tf_op jit(solution)/shard_map/pallas_call | solution.py:740
  114.0 0.0 copy-start
  114.0 1.8 %copy.16 = bf16[1,512,384]{2,1,0:T(8,128)(2,1)} copy(bf16[1,512,384]{2,1,0:T(8,128)(2,1)} %bitcast.6) | data formatting | bytes 786432
  115.8 0.0 copy-done
  115.8 0.6 copy.17
Async XLA Ops:
  114.0 1.8 %copy-start = (bf16[4,1024]{1,0:T(4,128)(2,1)S(1)}, bf16[4,1024]{1,0:T(4,128)(2,1)}, u32[]{:S(2)}) copy-start(bf16[4,1024]{1,0:T(4,128)(2,1)} %get-tuple-element.5) | copy-start | bytes 24580

commit v4 on v3

--- a/solution.py
+++ b/solution.py
@@ -20,7 +20,7 @@
 BF16 = jnp.bfloat16
 W_PIECES = 4
 W_START = 8
-W_RELAY = 1
+PAIR_LAG = 2
 RELAY_LAG = 8
 OWNER_LAG = 12
 
@@ -32,11 +32,11 @@
 SEGMENTS = [
     unit(0, 0),
     unit(1, 0),
-    unit(2, 0),
-    unit(3, 0) + unit(0, 1, 2) + unit(1, 1, 2),
-    unit(4, 0) + unit(2, 1, 2) + unit(3, 1, 2) + unit(4, 1, 2),
-    unit(5, 0, 1, 2) + unit(0, 3) + unit(1, 3) + unit(2, 3) + unit(3, 3) + unit(4, 3),
-    unit(5, 3) + unit(6, 3, 1, 2, 0),
+    unit(2, 0) + unit(0, 1, 2) + unit(1, 1, 2),
+    unit(3, 0) + unit(2, 1, 2) + unit(3, 1, 2),
+    unit(0, 3) + unit(4, 0, 1) + unit(1, 3) + unit(4, 2) + unit(2, 3) + unit(3, 3) + unit(4, 3),
+    unit(5, 3, 1, 2, 0),
+    unit(6, 3, 1, 2, 0),
     unit(7, 3, 1, 2, 0),
 ]
 UNITS = sum(SEGMENTS, [])
@@ -47,10 +47,6 @@
 
 def matmul_nt(a, b):
     return lax.dot_general(a, b, (((1,), (1,)), ((), ())), preferred_element_type=F32)
-
-
-def matmul_tn(a, b):
-    return lax.dot_general(a, b, (((0,), (0,)), ((), ())), preferred_element_type=F32)
 
 
 def remote(src, dst, send_sem, recv_sem, **target):
@@ -164,23 +160,41 @@
     greet(tp=sibling)
     greet(pool=1 - pool_at)
 
-    @pl.when(z > 0)
-    def _():
-        greet(seq=me - NX)
-
-    @pl.when(z < nz - 1)
-    def _():
-        greet(seq=me + NX)
+    around = 0
+    for distance in (1, 2):
+        for sign in (-1, 1):
+            there = (z + sign * distance >= 0) & (z + sign * distance < nz)
+            around = around + jnp.where(there, 1, 0)
+
+            @pl.when(there)
+            def _():
+                greet(seq=me + sign * distance * NX)
 
     load_k.wait()
     load_v.wait()
-    pl.semaphore_wait(barrier, 8 + jnp.where(z > 0, 1, 0) + jnp.where(z < nz - 1, 1, 0))
-
-    def kz_copy(zb, which, direction, target):
+    pl.semaphore_wait(barrier, 8 + around)
+
+    def kz_copy(zb, which, direction, distance):
         slot = kv.at[zb * NX + x, which]
         return remote(
-            slot, slot, kz_send.at[direction, zb, which], kz_recv.at[zb, which], seq=target
+            slot,
+            slot,
+            kz_send.at[direction, zb, which * 2 + distance - 1],
+            kz_recv.at[zb, which],
+            seq=me + (1 - 2 * direction) * distance * NX,
         )
+
+    def kz_sends(zb, direction, act):
+        travelled = (z - zb) * (1 - 2 * direction)
+        for which in range(2):
+            for distance in (1, 2):
+                target = z + (1 - 2 * direction) * distance
+
+                @pl.when(
+                    (travelled >= 0) & ((travelled & 1) == 0) & (target >= 0) & (target < nz)
+                )
+                def _():
+                    act(kz_copy(zb, which, direction, distance))
 
     def kx_copy(zb, xb, direction, target):
         slot = kv.at[zb * NX + xb]
@@ -263,6 +277,7 @@
     def attend(zb, diagonal):
         keys = kv[pl.ds(zb * NX, NX), 0].reshape(NX * span, HD)
         values = kv[pl.ds(zb * NX, NX), 1].reshape(NX * span, HD)
+        turned = jnp.transpose(values)
         pages = [span_ref[pool_at, zb * NX + j] for j in range(NX)]
         if diagonal:
             ahead = lax.broadcasted_iota(jnp.int32, (span, width), 0) - (
@@ -300,7 +315,9 @@
                 weights.append(jnp.exp2((block - base) * FACTOR))
                 sums.append(jnp.sum(weights[-1], axis=0, keepdims=True))
             total = (sums[0] + sums[1]) + (sums[2] + sums[3])
-            update = matmul_tn(values, jnp.concatenate(weights, axis=0).astype(BF16))
+            update = jnp.dot(
+                turned, jnp.concatenate(weights, axis=0).astype(BF16), preferred_element_type=F32
+            )
             if not diagonal:
                 fade = jnp.exp2((old_high - new_high) * FACTOR)
                 total = total + total_of[pair, 0:1] * fade
@@ -309,7 +326,7 @@
             total_of[pair, 0:1] = total
             accum[pair] = update
 
-    lag = 1 + jnp.where((z > 0) & (z < nz - 1), 1, 0) + jnp.where((z > 1) & (z < nz - 2), 1, 0)
+    lag = 1 + jnp.where((z > 1) & (z < nz - 2), 1, 0)
 
     load_q.wait()
     for pair in range(REPEAT // 2):
@@ -324,23 +341,16 @@
     def gather_step(t, carry):
         low, high = z - t, z + t
 
-        for which in range(2):
-
-            @pl.when((t > 0) & (low >= 0))
-            def _():
-                kz_copy(low, which, 0, me).wait_recv()
-
-            @pl.when((low >= 0) & (z < nz - 1))
-            def _():
-                kz_copy(low, which, 0, me + NX).start()
-
-            @pl.when((t > 0) & (high < nz))
-            def _():
-                kz_copy(high, which, 1, me).wait_recv()
-
-            @pl.when((high < nz) & (z > 0))
-            def _():
-                kz_copy(high, which, 1, me - NX).start()
+        for zb, direction in ((low, 0), (high, 1)):
+
+            @pl.when((zb >= 0) & (zb < nz))
+            def _():
+                @pl.when(t > 0)
+                def _():
+                    for which in range(2):
+                        kz_copy(zb, which, direction, 1).wait_recv()
+
+                kz_sends(zb, direction, lambda copy: copy.start())
 
         @pl.when(low >= 0)
         def _():
@@ -474,27 +484,40 @@
         ].astype(BF16)
     pool_copy = remote(dec_out, dec_in, pool_send.at[0], pool_recv.at[0], pool=1 - pool_at)
     pool_copy.start()
+    relay_weight(0)
 
     edge = jnp.minimum(z, nz - 1 - z)
 
-    def look_up(table, index):
-        value = jnp.int32(table[-1])
-        for n in reversed(range(len(table) - 1)):
-            value = jnp.where(index <= n, table[n], value)
-        return value
+    def bits(value, shift, mask):
+        return lax.shift_right_logical(value, shift) & mask
+
+    def unit_code(index):
+        words = [
+            sum(code << 8 * n for n, code in enumerate(UNITS[i : i + 4]))
+            for i in range(0, len(UNITS), 4)
+        ]
+        values = [jnp.int32(word) for word in words]
+        level = 2
+        while len(values) > 1:
+            odd = bits(index, level, 1) == 1
+            values = [
+                jnp.where(odd, values[n + 1], values[n]) for n in range(0, len(values), 2)
+            ]
+            level += 1
+        return bits(values[0], (index & 3) * 8, 255)
 
     def place_of(unit):
-        code = look_up(UNITS, unit)
-        k, turn = code // 4, code % 4
-        near = (k + 1) // 2
-        paired = jnp.where(k % 2 == 1, z - near, z + near)
+        code = unit_code(unit)
+        k, turn = bits(code, 2, 7), code & 3
+        near = bits(k + 1, 1, 7)
+        paired = jnp.where((k & 1) == 1, z - near, z + near)
         beyond = jnp.where(z < nz // 2, z + k - edge, z - k + edge)
         zb = jnp.where(k <= 2 * edge, paired, beyond)
-        quarter = (x + jnp.where(turn == 1, 3, jnp.where(turn == 2, 1, jnp.where(turn == 3, 2, 0)))) % NX
-        owner = zb // 2
-        toward = 1 - 2 * (quarter % 2)
-        rank = ((y - owner) * toward + 2 * ny) % ny
-        return zb % 2 == core, zb, quarter, owner, toward, rank, owner * NX + quarter
+        quarter = (x + turn + jnp.where(turn == 1, 2, jnp.where(turn == 0, 0, 3))) & 3
+        owner = bits(zb, 1, 7)
+        toward = 1 - 2 * (quarter & 1)
+        rank = ((y - owner) * toward + 4) & 3
+        return (zb & 1) == core, zb, quarter, owner, toward, rank, owner * NX + quarter
 
     def core_copy(slot):
         return remote(
@@ -537,7 +560,7 @@
             @pl.when(rank == 2)
             def _():
                 y_copy(
-                    slot, relay_in.at[quarter], relay_recv.at[quarter], (owner + toward + ny) % ny
+                    slot, relay_in.at[quarter], relay_recv.at[quarter], (owner + toward + 4) & 3
                 ).start()
 
             @pl.when(rank == 3)
@@ -560,7 +583,7 @@
         return carry
 
     def x_copy(quarter, source, target):
-        distance = (target + NX - source) % NX
+        distance = (target + NX - source) & 3
         return remote(
             x_out.at[quarter],
             x_in.at[source],
@@ -602,19 +625,20 @@
     def clipped(value):
         return jnp.clip(value, 0, count)
 
-    def flushing(unit):
-        return (unit >= count) | ((edge == 0) & ((unit == STEP_AT[6]) | (unit == STEP_AT[7])))
-
     def pairs_by(unit):
-        return clipped(jnp.where(unit >= count, unit, unit - 1 + jnp.where(flushing(unit), 1, 0)))
+        done = jnp.where(unit >= count, unit, unit - PAIR_LAG)
+        for at in STEP_AT[7:]:
+            done = jnp.where((edge == 0) & (unit >= at), jnp.maximum(done, at), done)
+        return clipped(done)
+
+    last = STEP_AT[-1]
 
     def relays_by(unit):
-        late = jnp.where(unit >= STEP_AT[7], count - 4 + unit - count, unit - RELAY_LAG)
-        return clipped(late)
+        return clipped(jnp.where(unit >= last, unit - 4, unit - RELAY_LAG))
 
     def owners_by(unit):
-        late = jnp.where(unit > count, count - 5 + unit - count, unit - OWNER_LAG)
-        return clipped(late)
+        done = jnp.where((unit >= last) & (edge > 0), unit - 8, unit - OWNER_LAG)
+        return clipped(jnp.where(unit > count, unit - 4, done))
 
     def steps_by(unit):
         done = jnp.int32(0)
@@ -622,25 +646,26 @@
             at = jnp.int32(STEP_AT[t])
             if t == 5:
                 at = at - jnp.where((edge == 1) | (edge == 2), 2, 0)
-            if t == 6:
-                at = at - jnp.where(edge == 1, 2, 0)
             done = done + jnp.where(unit >= at, 1, 0)
         return done
 
     def advance(t, carry):
         z_step(t, 0)
 
-        @pl.when((t >= W_RELAY) & (t < W_RELAY + W_PIECES // 2))
-        def _():
-            relay_weight(t - W_RELAY)
+        @pl.when(t == 1)
+        def _():
+            relay_weight(1)
 
         return carry
 
     def unit_step(unit, carry):
-        lax.fori_loop(pairs_by(unit - 1), pairs_by(unit), pair_sum, 0)
-        lax.fori_loop(relays_by(unit - 1), relays_by(unit), relay_sum, 0)
-        lax.fori_loop(owners_by(unit - 1), owners_by(unit), owner_sum, 0)
-        lax.fori_loop(steps_by(unit - 1) + 1, steps_by(unit) + 1, advance, 0)
+        pairs, relays, owners, z_steps = carry
+        new_pairs, new_relays = pairs_by(unit), relays_by(unit)
+        new_owners, new_steps = owners_by(unit), steps_by(unit)
+        lax.fori_loop(pairs, new_pairs, pair_sum, 0)
+        lax.fori_loop(relays, new_relays, relay_sum, 0)
+        lax.fori_loop(owners, new_owners, owner_sum, 0)
+        lax.fori_loop(z_steps + 1, new_steps + 1, advance, 0)
 
         @pl.when(unit == NEAR_AT)
         def _():
@@ -654,10 +679,10 @@
         def _():
             project(unit)
 
-        return carry
+        return (new_pairs, new_relays, new_owners, new_steps)
 
     load_r.wait()
-    lax.fori_loop(0, count + 6, unit_step, 0)
+    lax.fori_loop(0, count + 6, unit_step, (jnp.int32(0),) * 4)
 
     for distance in range(1, NX):
         source = (x + NX - distance) % NX
@@ -668,16 +693,17 @@
     dec_ref[...] = dec_in[:steps, :]
 
     def drain(zb, carry):
+        for direction in range(2):
+            kz_sends(zb, direction, lambda copy: copy.wait_send())
+
         @pl.when((zb <= z) & (z < nz - 1))
         def _():
             for s in range(2):
-                kz_copy(zb, s, 0, me).wait_send()
                 az_copy(zb, s, 0, me).wait_send()
 
         @pl.when((zb >= z) & (z > 0))
         def _():
             for s in range(2):
-                kz_copy(zb, s, 1, me).wait_send()
                 az_copy(zb, s, 1, me).wait_send()
 
         kx_copy(zb, x, 0, right).wait_send()
@@ -771,7 +797,7 @@
             pltpu.VMEM((16, features), BF16),
             pltpu.VMEM((16, features), BF16),
             dma((8,)),
-            dma((2, nz, 2)),
+            dma((2, nz, 4)),
             dma((nz, 2)),
             dma((2, nz)),
             dma((2, nz)),

time: 117 us -> 114 us (0.974)
  the two profiles are of different devices: /device:TPU:27 before, /device:TPU:89 now
where the time goes in v4:
time: 114 us
  Pallas kernels  111 us (97%)
  local copies, waits for them, and re-layouts  2.39 us (2%)
    pallas_call x1, Pallas kernels, per_device(): pl.pallas_call(kernel, out_shape=(jax.ShapeDtypeStruct(residual.shape[1:]...  111 us
    unnamed x4, local copies, waits for them, and re-layouts  2.39 us

profile of v4, /device:TPU:89, one launch (start us, length us, event | category | flops | bytes accessed | tf_op | source)
XLA Modules:
  0.0 113.6 jit_solution(4910725844978040779)
XLA Ops:
  0.6 110.6 %shard_map.131 = (bf16[512,384]{1,0:T(8,128)(2,1)}, bf16[4,1024]{1,0:T(4,128)(2,1)}) custom-call(s32[2,32]{1,0:T(2,128)} %span_ref.1, s32[2,8]{1,0:T(2,128)} %counts_ref.1, s32[2,8]{1,0:T(2,128)} %tails_ref.1, s32[2,8]{1,0:T(2,128)} %dest_ref.1, bf16[2,8,4,1024]{3,2,1,0:T(4,128)(2,1)} %dq_hbm.1, bf16[2,8,4,128]{3,2,1,0:T(4,128)(2,1)} %dk_hbm.1, ...), custom_call_target="tpu_custom_call" | custom-call | tf_op jit(solution)/shard_map/pallas_call | solution.py:766
  111.2 0.0 copy-start
  111.3 1.8 %copy.16 = bf16[1,512,384]{2,1,0:T(8,128)(2,1)} copy(bf16[1,512,384]{2,1,0:T(8,128)(2,1)} %bitcast.6) | data formatting | bytes 786432
  113.0 0.0 copy-done
  113.0 0.6 copy.17
Async XLA Ops:
  111.2 1.8 %copy-start = (bf16[4,1024]{1,0:T(4,128)(2,1)S(1)}, bf16[4,1024]{1,0:T(4,128)(2,1)}, u32[]{:S(2)}) copy-start(bf16[4,1024]{1,0:T(4,128)(2,1)} %get-tuple-element.5) | copy-start | bytes 24580

commit v5 on v4

--- a/solution.py
+++ b/solution.py
@@ -634,7 +634,7 @@
     last = STEP_AT[-1]
 
     def relays_by(unit):
-        return clipped(jnp.where(unit >= last, unit - 4, unit - RELAY_LAG))
+        return clipped(jnp.where(unit >= last + 2, unit - 4, unit - RELAY_LAG))
 
     def owners_by(unit):
         done = jnp.where((unit >= last) & (edge > 0), unit - 8, unit - OWNER_LAG)

time: 114 us -> 113 us (level)
  the two profiles are of different devices: /device:TPU:89 before, /device:TPU:57 now
where the time goes in v5:
time: 113 us
  Pallas kernels  110 us (97%)
  local copies, waits for them, and re-layouts  2.39 us (2%)
    pallas_call x1, Pallas kernels, per_device(): pl.pallas_call(kernel, out_shape=(jax.ShapeDtypeStruct(residual.shape[1:]...  110 us
    unnamed x4, local copies, waits for them, and re-layouts  2.39 us

profile of v5, /device:TPU:57, one launch (start us, length us, event | category | flops | bytes accessed | tf_op | source)
XLA Modules:
  0.0 112.8 jit_solution(14190417119010334130)
XLA Ops:
  0.6 109.8 %shard_map.131 = (bf16[512,384]{1,0:T(8,128)(2,1)}, bf16[4,1024]{1,0:T(4,128)(2,1)}) custom-call(s32[2,32]{1,0:T(2,128)} %span_ref.1, s32[2,8]{1,0:T(2,128)} %counts_ref.1, s32[2,8]{1,0:T(2,128)} %tails_ref.1, s32[2,8]{1,0:T(2,128)} %dest_ref.1, bf16[2,8,4,1024]{3,2,1,0:T(4,128)(2,1)} %dq_hbm.1, bf16[2,8,4,128]{3,2,1,0:T(4,128)(2,1)} %dk_hbm.1, ...), custom_call_target="tpu_custom_call" | custom-call | tf_op jit(solution)/shard_map/pallas_call | solution.py:766
  110.4 0.0 copy-start
  110.4 1.8 %copy.16 = bf16[1,512,384]{2,1,0:T(8,128)(2,1)} copy(bf16[1,512,384]{2,1,0:T(8,128)(2,1)} %bitcast.6) | data formatting | bytes 786432
  112.2 0.0 copy-done
  112.2 0.6 copy.17
Async XLA Ops:
  110.4 1.8 %copy-start = (bf16[4,1024]{1,0:T(4,128)(2,1)S(1)}, bf16[4,1024]{1,0:T(4,128)(2,1)}, u32[]{:S(2)}) copy-start(bf16[4,1024]{1,0:T(4,128)(2,1)} %get-tuple-element.5) | copy-start | bytes 24580

commit v6 on v5

--- a/solution.py
+++ b/solution.py
@@ -637,7 +637,7 @@
         return clipped(jnp.where(unit >= last + 2, unit - 4, unit - RELAY_LAG))
 
     def owners_by(unit):
-        done = jnp.where((unit >= last) & (edge > 0), unit - 8, unit - OWNER_LAG)
+        done = jnp.where(unit >= last + 2, unit - 8, unit - OWNER_LAG)
         return clipped(jnp.where(unit > count, unit - 4, done))
 
     def steps_by(unit):

time: 113 us -> 113 us (level)
  the two profiles are of different devices: /device:TPU:57 before, /device:TPU:24 now
where the time goes in v6:
time: 113 us; the launch traced here: 111 us
  Pallas kernels  108 us (96%)
  local copies, waits for them, and re-layouts  2.39 us (2%)
    pallas_call x1, Pallas kernels, per_device(): pl.pallas_call(kernel, out_shape=(jax.ShapeDtypeStruct(residual.shape[1:]...  108 us
    unnamed x4, local copies, waits for them, and re-layouts  2.39 us

profile of v6, /device:TPU:24, one launch (start us, length us, event | category | flops | bytes accessed | tf_op | source)
XLA Modules:
  0.0 110.6 jit_solution(11312712820763339269)
XLA Ops:
  0.6 107.5 %shard_map.131 = (bf16[512,384]{1,0:T(8,128)(2,1)}, bf16[4,1024]{1,0:T(4,128)(2,1)}) custom-call(s32[2,32]{1,0:T(2,128)} %span_ref.1, s32[2,8]{1,0:T(2,128)} %counts_ref.1, s32[2,8]{1,0:T(2,128)} %tails_ref.1, s32[2,8]{1,0:T(2,128)} %dest_ref.1, bf16[2,8,4,1024]{3,2,1,0:T(4,128)(2,1)} %dq_hbm.1, bf16[2,8,4,128]{3,2,1,0:T(4,128)(2,1)} %dk_hbm.1, ...), custom_call_target="tpu_custom_call" | custom-call | tf_op jit(solution)/shard_map/pallas_call | solution.py:766
  108.2 0.0 copy-start
  108.2 1.8 %copy.16 = bf16[1,512,384]{2,1,0:T(8,128)(2,1)} copy(bf16[1,512,384]{2,1,0:T(8,128)(2,1)} %bitcast.6) | data formatting | bytes 786432
  110.0 0.0 copy-done
  110.0 0.6 copy.17
Async XLA Ops:
  108.2 1.8 %copy-start = (bf16[4,1024]{1,0:T(4,128)(2,1)S(1)}, bf16[4,1024]{1,0:T(4,128)(2,1)}, u32[]{:S(2)}) copy-start(bf16[4,1024]{1,0:T(4,128)(2,1)} %get-tuple-element.5) | copy-start | bytes 24580
